TPU v7x, 256 devices: a whole 4x4x8 slice. The times are simulated.
256 devices in a mesh: blk: 32 (over x, y, z_hi), kv: 8 (over z_lo, core).
Axes of the slice: x: 4, y: 4, z: 8 (z_hi: 2, z_lo: 4; z = z_hi * 4 + z_lo), core: 2. Of those that a mesh axis runs over, the one named last changes fastest.
Arguments:
- queries: bfloat16 [16384, 1024], P(('blk', 'kv')), may hold values from -16 to 16
- keys: bfloat16 [16384, 1024], P(('blk', 'kv')), may hold values from -16 to 16
- values: bfloat16 [16384, 1024], P(('blk', 'kv')), may hold values from -6 to 6
- w_out: bfloat16 [1024, 1024], replicated, may hold values from -0.1875 to 0.1875
Outputs:
- encoded: bfloat16 [16384, 1024], P(('blk', 'kv'))
All inputs are finite; a program needn't handle non-finite values.
Results may differ from a plain program's by a relative error of at most 0.01.
Values may be sent and summed in bfloat16 or wider, within the bound.
No kernel may reach another device: no remote copies, remote signals or barrier semaphores. Data moves between devices by JAX's collectives and lax.ppermute only.
A program may use at most 128 MiB of HBM per device.

v0:
```python
import functools

import jax
import jax.numpy as jnp
from jax import lax
from jax.experimental import pallas as pl
from jax.experimental.pallas import tpu as pltpu
from jax.sharding import Mesh, PartitionSpec as P

HEADS = 16
HEAD_DIM = 64
LANES = 128
STAT = HEAD_DIM
SHIFT = LANES - 1
LOG2E = 1.4426950408889634
BIG = 2.0**100
LOWEST = -1e30
ROW_BLOCK = 512

NT = (((1,), (1,)), ((), ()))


def pack_kernel(q_hbm, k_hbm, v_hbm, out_ref, q_ref, k_ref, v_ref, sem):
    rows = q_ref.shape[0]
    half = rows // 2
    copies = [
        pltpu.make_async_copy(source, target, sem.at[n])
        for n, (source, target) in enumerate(((k_hbm, k_ref), (v_hbm, v_ref), (q_hbm, q_ref)))
    ]
    for copy in copies:
        copy.start()
    for copy in copies:
        copy.wait()
    for head in range(HEADS):
        cols = slice(head * HEAD_DIM, (head + 1) * HEAD_DIM)
        out_ref[head, :rows, :] = jnp.concatenate([k_ref[:, cols], v_ref[:, cols]], axis=1)
        q = q_ref[:, cols]
        out_ref[head, rows:, :] = jnp.concatenate([q[:half], q[half:]], axis=1)


def split_queries(q):
    stacked = jnp.concatenate([q[:, :HEAD_DIM], q[:, HEAD_DIM:]], axis=0).astype(jnp.float32)
    scaled = stacked * (LOG2E * HEAD_DIM**-0.5)
    high = scaled.astype(jnp.bfloat16)
    low = (scaled - high.astype(jnp.float32)).astype(jnp.bfloat16)
    return jnp.concatenate([high, low], axis=1)


def keys_twice(kv):
    return jnp.concatenate([kv[:, :HEAD_DIM], kv[:, :HEAD_DIM]], axis=1)


def values_and_one(kv):
    lane = lax.broadcasted_iota(jnp.int32, (kv.shape[0], HEAD_DIM), 1)
    one = jnp.where(lane == 0, 1.0, 0.0).astype(kv.dtype)
    return jnp.concatenate([kv[:, HEAD_DIM:], one], axis=1)


def with_shift(acc, shift):
    lane = lax.broadcasted_iota(jnp.int32, acc.shape, 1)
    return jnp.where(lane == SHIFT, shift, acc)


def scores(q_ref, rows, keys):
    return lax.dot_general(q_ref[rows, :], keys, NT, preferred_element_type=jnp.float32)


def first_kernel(q_own_ref, q_other_ref, kv_ref, q_ref, acc_ref):
    heads, rows, _ = q_own_ref.shape
    count = 2 * heads * rows
    q_ref[:count, :] = split_queries(q_own_ref[...].reshape(heads * rows, LANES))
    q_ref[count:, :] = split_queries(q_other_ref[...].reshape(heads * rows, LANES))
    keys, values = keys_twice(kv_ref[...]), values_and_one(kv_ref[...])

    def one(rows):
        s = scores(q_ref, rows, keys)
        shift = jnp.max(s, axis=1, keepdims=True)
        p = jnp.exp2(s - shift).astype(jnp.bfloat16)
        acc_ref[rows, :] = with_shift(jnp.dot(p, values, preferred_element_type=jnp.float32), shift)

    each_row_block(q_ref, one)


def each_row_block(q_ref, step):
    def body(i, carry):
        step(pl.ds(pl.multiple_of(i * ROW_BLOCK, ROW_BLOCK), ROW_BLOCK))
        return carry

    lax.fori_loop(0, q_ref.shape[0] // ROW_BLOCK, body, 0)


def step_kernel(q_ref, kv_ref, acc_in_ref, acc_ref):
    keys, values = keys_twice(kv_ref[...]), values_and_one(kv_ref[...])

    def one(rows):
        acc = acc_in_ref[rows, :]
        p = jnp.exp2(scores(q_ref, rows, keys) - acc[:, SHIFT:]).astype(jnp.bfloat16)
        acc_ref[rows, :] = acc + jnp.dot(p, values, preferred_element_type=jnp.float32)

    each_row_block(q_ref, one)


def last_kernel(q_ref, kv_ref, acc_in_ref, *refs):
    kv_refs, (acc_ref, kv_buf, sem) = refs[:-3], refs[-3:]
    step_kernel(q_ref, kv_ref, acc_in_ref, acc_ref)
    outside = jnp.where(acc_ref[...] < BIG, 0.0, 1.0)
    fine = jnp.max(jnp.sum(outside, axis=0, keepdims=True)) < 0.5

    @pl.when(jnp.logical_not(fine))
    def _():
        acc_ref[...] = with_shift(jnp.zeros_like(acc_ref), LOWEST)
        for other_kv_ref in kv_refs:
            copy = pltpu.make_async_copy(other_kv_ref, kv_buf, sem)
            copy.start()
            copy.wait()
            redo_block(q_ref, kv_buf, acc_ref)


def redo_block(q_ref, kv_ref, acc_ref):
    keys, values = keys_twice(kv_ref[...]), values_and_one(kv_ref[...])

    def one(rows):
        s = scores(q_ref, rows, keys)
        acc = acc_ref[rows, :]
        before = acc[:, SHIFT:]
        highest = jnp.maximum(jnp.max(s, axis=1, keepdims=True), before)
        p = jnp.exp2(s - highest).astype(jnp.bfloat16)
        contrib = jnp.dot(p, values, preferred_element_type=jnp.float32)
        acc_ref[rows, :] = with_shift(acc * jnp.exp2(before - highest) + contrib, highest)

    each_row_block(q_ref, one)


def merge_kernel(own_ref, other_ref, out_ref):
    own, other = own_ref[...], other_ref[...]
    a, b = own[:, SHIFT:], other[:, SHIFT:]
    top = jnp.maximum(a, b)
    both = own * jnp.exp2(a - top) + other * jnp.exp2(b - top)
    attended = (both[:, :HEAD_DIM] / both[:, STAT : STAT + 1]).astype(jnp.bfloat16)
    half = attended.shape[0] // 2
    out_ref[...] = jnp.concatenate([attended[:half], attended[half:]], axis=1).reshape(
        out_ref.shape
    )


def project_kernel(heads_ref, w_ref, out_ref):
    left = [heads_ref[h][:, :HEAD_DIM] for h in range(HEADS)]
    right = [heads_ref[h][:, HEAD_DIM:] for h in range(HEADS)]
    attended = jnp.concatenate(
        [jnp.concatenate(left, axis=1), jnp.concatenate(right, axis=1)], axis=0
    )
    out_ref[...] = jnp.dot(attended, w_ref[...], preferred_element_type=jnp.float32).astype(
        jnp.bfloat16
    )


def call(kernel, *shapes, vmem=24, **more):
    return pl.pallas_call(
        kernel,
        out_shape=shapes if len(shapes) > 1 else shapes[0],
        compiler_params=pltpu.CompilerParams(vmem_limit_bytes=vmem * 2**20),
        **more,
    )


def on_device(q, k, v, w_out):
    rows, width = q.shape
    half = rows // 2
    bf16, f32 = jnp.bfloat16, jnp.float32
    shape = jax.ShapeDtypeStruct
    vmem = pl.BlockSpec(memory_space=pltpu.VMEM)
    anywhere = pl.BlockSpec(memory_space=pl.ANY)

    packed = call(
        pack_kernel,
        shape((HEADS, rows + half, LANES), bf16),
        vmem=56,
        in_specs=[anywhere] * 3,
        out_specs=vmem,
        scratch_shapes=[pltpu.VMEM((rows, width), bf16)] * 3 + [pltpu.SemaphoreType.DMA((3,))],
    )(q, k, v)
    mine = lax.all_to_all(packed, ("x", "y"), 0, 0, tiled=True)
    swap = [(0, 1), (1, 0)]
    count = HEADS * rows
    kv = mine[:, :rows].reshape(count, LANES)

    deep = lax.axis_size("zh") * lax.axis_size("zl")
    pairings = (
        lambda z: z ^ 1,
        lambda z: (z + 1) % deep if z % 2 else (z - 1) % deep,
    )

    def exchanged(block, hop):
        pairs = [
            (2 * z + c, 2 * pairings[(hop + c) % 2](z) + c) for z in range(deep) for c in range(2)
        ]
        return lax.ppermute(block, ("zh", "zl", "c"), pairs)

    def cost(blocks):
        return pl.CostEstimate(
            flops=2 * 2 * 2 * count * count * 2 * LANES * blocks,
            bytes_accessed=4 * 2**20,
            transcendentals=2 * count * count * blocks,
        )

    q_shape, acc_shape = shape((2 * count, LANES), bf16), shape((2 * count, LANES), f32)
    chains = [exchanged(kv, 0)]
    partners = lax.ppermute(mine, "c", swap)
    chains.append(exchanged(partners[:, :rows].reshape(count, LANES), 0))
    q_all, acc = call(first_kernel, q_shape, acc_shape, cost_estimate=cost(1))(
        mine[:, rows:], partners[:, rows:], kv
    )
    blocks = [kv]
    for hop in range(1, deep // 2):
        for n in range(2):
            now, acc = lax.optimization_barrier((chains[n], acc))
            blocks.append(now)
            if n == 0 or hop + 1 < deep // 2:
                chains[n] = exchanged(now, hop)
            acc = call(
                step_kernel, acc_shape, cost_estimate=cost(1), input_output_aliases={2: 0}
            )(q_all, now, acc)
    blocks.append(chains[0])
    acc = call(
        last_kernel,
        acc_shape,
        in_specs=[vmem] * 3 + [anywhere] * len(blocks),
        out_specs=vmem,
        scratch_shapes=[pltpu.VMEM((count, LANES), bf16), pltpu.SemaphoreType.DMA],
        cost_estimate=cost(1),
        input_output_aliases={2: 0},
    )(q_all, chains[0], acc, *blocks)
    arrived = lax.ppermute(acc[count:], "c", swap)
    own = acc[:count]
    attended = call(merge_kernel, shape((HEADS, half, LANES), bf16))(own, arrived)
    heads = lax.all_to_all(attended, ("x", "y"), 0, 0, tiled=True)
    return call(project_kernel, shape((rows, width), bf16))(heads, w_out)


def solution(mesh):
    axes = ("x", "y", "zh", "zl", "c")
    fine = Mesh(mesh.devices.reshape(4, 4, 2, 4, 2), axes)
    return jax.shard_map(
        on_device,
        mesh=fine,
        in_specs=(P(axes, None), P(axes, None), P(axes, None), P()),
        out_specs=P(axes, None),
        check_vma=False,
    )
```

profile of v0, /device:TPU:1, one launch (start us, length us, event | category | flops | bytes accessed | tf_op | source)
XLA Modules:
  0.0 117.5 jit_solution(15960203025565595602)
XLA Ops:
  0.0 2.0 %shard_map.46 = bf16[16,96,128]{2,1,0:T(8,128)(2,1)} custom-call(bf16[64,1024]{1,0:T(8,128)(2,1)} %q_hbm.1, bf16[64,1024]{1,0:T(8,128)(2,1)} %k_hbm.1, bf16[64,1024]{1,0:T(8,128)(2,1)} %v_hbm.1), custom_call_target="tpu_custom_call" | custom-call | tf_op jit(solution)/shard_map/pallas_call | solution.py:174
  2.0 15.9 %all_to_all.10 = bf16[16,96,128]{2,1,0:T(8,128)(2,1)S(1)} all-to-all(bf16[16,96,128]{2,1,0:T(8,128)(2,1)} %shard_map.46), channel_id=1, replica_groups=mesh['x'=4,'y'=4,'zh'=2,'zl'=4,'c'=2] {'x','y'}, dimensions={0} | all-to-all | bytes 786432 | tf_op jit(solution)/shard_map/all_to_all | solution.py:182
  17.8 2.5 %collective-permute-start = (bf16[16,96,128]{2,1,0:T(8,128)(2,1)S(1)}, bf16[16,96,128]{2,1,0:T(8,128)(2,1)S(1)}, u32[]{:S(2)}, u32[]{:S(2)}) collective-permute-start(bf16[16,96,128]{2,1,0:T(8,128)(2,1)S(1)} %all_to_all.10), channel_id=1, source_target_pairs={{0,1},{1,0},{2,3},{3,2},{4,5},{5,4},{6,7},{7,6},{8,9},{9,8},{10,11... | collective-permute-start | bytes 1179656 | tf_op jit(solution)/shard_map/ppermute | solution.py:208
  20.4 5.7 %collective-permute-start.1 = (bf16[1024,128]{1,0:T(8,128)(2,1)S(1)}, bf16[1024,128]{1,0:T(8,128)(2,1)S(1)}, u32[]{:S(2)}, u32[]{:S(2)}) collective-permute-start(bf16[1024,128]{1,0:T(8,128)(2,1)S(1)} %bitcast.2), channel_id=1, source_target_pairs={{0,2},{1,15},{2,0},{3,5},{4,6},{5,3},{6,4},{7,9},{8,10},{9,7},{10,... | collective-permute-start | bytes 786440 | tf_op jit(solution)/shard_map/ppermute | solution.py:197
  26.0 0.0 collective-permute-done
  26.1 1.3 %collective-permute-start.3 = (bf16[1024,128]{1,0:T(8,128)(2,1)S(1)}, bf16[1024,128]{1,0:T(8,128)(2,1)S(1)}, u32[]{:S(2)}, u32[]{:S(2)}) collective-permute-start(bf16[1024,128]{1,0:T(8,128)(2,1)S(1)} %bitcast.5), channel_id=1, source_target_pairs={{0,2},{1,15},{2,0},{3,5},{4,6},{5,3},{6,4},{7,9},{8,10},{9,7},{10,... | collective-permute-start | bytes 786440 | tf_op jit(solution)/shard_map/ppermute | solution.py:197
  27.4 5.6 %shard_map.47 = (bf16[2048,128]{1,0:T(8,128)(2,1)S(1)}, f32[2048,128]{1,0:T(8,128)S(1)}) custom-call(bf16[16,32,128]{2,1,0:T(8,128)(2,1)S(1)} %slice.24.q_own_ref, bf16[16,32,128]{2,1,0:T(8,128)(2,1)S(1)} %slice.25.q_other_ref, bf16[1024,128]{1,0:T(8,128)(2,1)S(1)} %bitcast.3), custom_call_target="tpu_custom_call" | custom-call | flops 2147483648 | bytes 4194304 | tf_op jit(solution)/shard_map/pallas_call | solution.py:210
  33.0 0.0 collective-permute-done.1.kv_ref.refs_1_
  33.0 0.1 collective-permute-start.2
  33.1 3.1 %shard_map.48.acc_in_ref = f32[2048,128]{1,0:T(8,128)S(1)} custom-call(bf16[2048,128]{1,0:T(8,128)(2,1)S(1)} %get-tuple-element.19.q_ref, bf16[1024,128]{1,0:T(8,128)(2,1)S(1)} %collective-permute-done.1.kv_ref.refs_1_, f32[2048,128]{1,0:T(8,128)S(1)} %get-tuple-element.22.acc_in_ref), custom_call_target="tpu_custom_call", output_to_operand_aliasing={{}: (2, {})} | custom-call | flops 2147483648 | bytes 4194304 | tf_op jit(solution)/shard_map/pallas_call | solution.py:220
  36.2 0.0 collective-permute-done.3.kv_ref.refs_2_
  36.2 1.5 %collective-permute-start.5 = (bf16[1024,128]{1,0:T(8,128)(2,1)S(1)}, bf16[1024,128]{1,0:T(8,128)(2,1)S(1)}, u32[]{:S(2)}, u32[]{:S(2)}) collective-permute-start(bf16[1024,128]{1,0:T(8,128)(2,1)S(1)} %collective-permute-done.3.kv_ref.refs_2_), channel_id=1, source_target_pairs={{0,14},{1,3},{2,4},{3,1},{4,2},{5,7},{6,8},{7,5},{8,6},{9,11},{10,... | collective-permute-start | bytes 786440 | tf_op jit(solution)/shard_map/ppermute | solution.py:197
  37.7 3.1 %shard_map.49.acc_in_ref = f32[2048,128]{1,0:T(8,128)S(1)} custom-call(bf16[2048,128]{1,0:T(8,128)(2,1)S(1)} %get-tuple-element.19.q_ref, bf16[1024,128]{1,0:T(8,128)(2,1)S(1)} %collective-permute-done.3.kv_ref.refs_2_, f32[2048,128]{1,0:T(8,128)S(1)} %shard_map.48.acc_in_ref), custom_call_target="tpu_custom_call", output_to_operand_aliasing={{}: (2, {})} | custom-call | flops 2147483648 | bytes 4194304 | tf_op jit(solution)/shard_map/pallas_call | solution.py:220
  40.8 0.0 collective-permute-done.2.kv_ref.refs_3_
  40.8 1.5 %collective-permute-start.4 = (bf16[1024,128]{1,0:T(8,128)(2,1)S(1)}, bf16[1024,128]{1,0:T(8,128)(2,1)S(1)}, u32[]{:S(2)}, u32[]{:S(2)}) collective-permute-start(bf16[1024,128]{1,0:T(8,128)(2,1)S(1)} %collective-permute-done.2.kv_ref.refs_3_), channel_id=1, source_target_pairs={{0,2},{1,15},{2,0},{3,5},{4,6},{5,3},{6,4},{7,9},{8,10},{9,7},{10,... | collective-permute-start | bytes 786440 | tf_op jit(solution)/shard_map/ppermute | solution.py:197
  42.3 3.0 %shard_map.50.acc_in_ref = f32[2048,128]{1,0:T(8,128)S(1)} custom-call(bf16[2048,128]{1,0:T(8,128)(2,1)S(1)} %get-tuple-element.19.q_ref, bf16[1024,128]{1,0:T(8,128)(2,1)S(1)} %collective-permute-done.2.kv_ref.refs_3_, f32[2048,128]{1,0:T(8,128)S(1)} %shard_map.49.acc_in_ref), custom_call_target="tpu_custom_call", output_to_operand_aliasing={{}: (2, {})} | custom-call | flops 2147483648 | bytes 4194304 | tf_op jit(solution)/shard_map/pallas_call | solution.py:220
  45.4 0.0 collective-permute-done.5.kv_ref.refs_4_
  45.4 1.3 %collective-permute-start.7 = (bf16[1024,128]{1,0:T(8,128)(2,1)S(1)}, bf16[1024,128]{1,0:T(8,128)(2,1)S(1)}, u32[]{:S(2)}, u32[]{:S(2)}) collective-permute-start(bf16[1024,128]{1,0:T(8,128)(2,1)S(1)} %collective-permute-done.5.kv_ref.refs_4_), channel_id=1, source_target_pairs={{0,2},{1,15},{2,0},{3,5},{4,6},{5,3},{6,4},{7,9},{8,10},{9,7},{10,... | collective-permute-start | bytes 786440 | tf_op jit(solution)/shard_map/ppermute | solution.py:197
  46.7 3.0 %shard_map.51.acc_in_ref = f32[2048,128]{1,0:T(8,128)S(1)} custom-call(bf16[2048,128]{1,0:T(8,128)(2,1)S(1)} %get-tuple-element.19.q_ref, bf16[1024,128]{1,0:T(8,128)(2,1)S(1)} %collective-permute-done.5.kv_ref.refs_4_, f32[2048,128]{1,0:T(8,128)S(1)} %shard_map.50.acc_in_ref), custom_call_target="tpu_custom_call", output_to_operand_aliasing={{}: (2, {})} | custom-call | flops 2147483648 | bytes 4194304 | tf_op jit(solution)/shard_map/pallas_call | solution.py:220
  49.8 0.0 collective-permute-done.4.kv_ref.refs_5_
  49.8 0.1 collective-permute-start.6
  49.9 3.0 %shard_map.52.acc_in_ref = f32[2048,128]{1,0:T(8,128)S(1)} custom-call(bf16[2048,128]{1,0:T(8,128)(2,1)S(1)} %get-tuple-element.19.q_ref, bf16[1024,128]{1,0:T(8,128)(2,1)S(1)} %collective-permute-done.4.kv_ref.refs_5_, f32[2048,128]{1,0:T(8,128)S(1)} %shard_map.51.acc_in_ref), custom_call_target="tpu_custom_call", output_to_operand_aliasing={{}: (2, {})} | custom-call | flops 2147483648 | bytes 4194304 | tf_op jit(solution)/shard_map/pallas_call | solution.py:220
  52.9 0.0 collective-permute-done.7.kv_ref.refs_6_
  52.9 3.0 %shard_map.53.acc_in_ref = f32[2048,128]{1,0:T(8,128)S(1)} custom-call(bf16[2048,128]{1,0:T(8,128)(2,1)S(1)} %get-tuple-element.19.q_ref, bf16[1024,128]{1,0:T(8,128)(2,1)S(1)} %collective-permute-done.7.kv_ref.refs_6_, f32[2048,128]{1,0:T(8,128)S(1)} %shard_map.52.acc_in_ref), custom_call_target="tpu_custom_call", output_to_operand_aliasing={{}: (2, {})} | custom-call | flops 2147483648 | bytes 4194304 | tf_op jit(solution)/shard_map/pallas_call | solution.py:220
  56.0 0.0 collective-permute-done.6.kv_ref.refs_7_
  56.0 46.3 %shard_map.54 = f32[2048,128]{1,0:T(8,128)S(1)} custom-call(bf16[2048,128]{1,0:T(8,128)(2,1)S(1)} %get-tuple-element.19.q_ref, bf16[1024,128]{1,0:T(8,128)(2,1)S(1)} %collective-permute-done.6.kv_ref.refs_7_, f32[2048,128]{1,0:T(8,128)S(1)} %shard_map.53.acc_in_ref, bf16[1024,128]{1,0:T(8,128)(2,1)S(1)} %bitcast.4, ...), custom_call_target="tpu_custom_call", output_to_operand_aliasing={{}: (2, {})} | custom-call | flops 2147483648 | bytes 4194304 | tf_op jit(solution)/shard_map/pallas_call | solution.py:224
  102.3 0.0 copy-start
  102.3 0.1 fusion
  102.4 0.1 collective-permute-start.8
  102.5 1.9 %collective-permute-done.8.other_ref = f32[1024,128]{1,0:T(8,128)S(1)} collective-permute-done((f32[1024,128]{1,0:T(8,128)S(1)}, f32[1024,128]{1,0:T(8,128)S(1)}, u32[]{:S(2)}, u32[]{:S(2)}) %collective-permute-start.8) | collective-permute-done | bytes 524320 | tf_op jit(solution)/shard_map/ppermute | solution.py:233
  104.4 0.6 shard_map.55
  104.9 11.4 %all_to_all.11.heads_ref = bf16[16,32,128]{2,1,0:T(8,128)(2,1)S(1)} all-to-all(bf16[16,32,128]{2,1,0:T(8,128)(2,1)S(1)} %shard_map.55), channel_id=1, replica_groups=mesh['x'=4,'y'=4,'zh'=2,'zl'=4,'c'=2] {'x','y'}, dimensions={0} | all-to-all | bytes 262144 | tf_op jit(solution)/shard_map/all_to_all | solution.py:236
  116.4 0.0 copy-done
  116.4 1.2 %shard_map.56 = bf16[64,1024]{1,0:T(8,128)(2,1)} custom-call(bf16[16,32,128]{2,1,0:T(8,128)(2,1)S(1)} %all_to_all.11.heads_ref, bf16[1024,1024]{1,0:T(8,128)(2,1)S(1)} %copy-done), custom_call_target="tpu_custom_call" | custom-call | tf_op jit(solution)/shard_map/pallas_call | solution.py:237
  (4 shorter events, 0.1 us)
Async XLA Ops:
  17.8 8.2 %collective-permute-start = (bf16[16,96,128]{2,1,0:T(8,128)(2,1)S(1)}, bf16[16,96,128]{2,1,0:T(8,128)(2,1)S(1)}, u32[]{:S(2)}, u32[]{:S(2)}) collective-permute-start(bf16[16,96,128]{2,1,0:T(8,128)(2,1)S(1)} %all_to_all.10), channel_id=1, source_target_pairs={{0,1},{1,0},{2,3},{3,2},{4,5},{5,4},{6,7},{7,6},{8,9},{9,8},{10,11... | collective-permute-start | bytes 1179656 | tf_op jit(solution)/shard_map/ppermute | solution.py:208
  20.4 12.6 %collective-permute-start.1 = (bf16[1024,128]{1,0:T(8,128)(2,1)S(1)}, bf16[1024,128]{1,0:T(8,128)(2,1)S(1)}, u32[]{:S(2)}, u32[]{:S(2)}) collective-permute-start(bf16[1024,128]{1,0:T(8,128)(2,1)S(1)} %bitcast.2), channel_id=1, source_target_pairs={{0,2},{1,15},{2,0},{3,5},{4,6},{5,3},{6,4},{7,9},{8,10},{9,7},{10,... | collective-permute-start | bytes 786440 | tf_op jit(solution)/shard_map/ppermute | solution.py:197
  26.1 10.1 %collective-permute-start.3 = (bf16[1024,128]{1,0:T(8,128)(2,1)S(1)}, bf16[1024,128]{1,0:T(8,128)(2,1)S(1)}, u32[]{:S(2)}, u32[]{:S(2)}) collective-permute-start(bf16[1024,128]{1,0:T(8,128)(2,1)S(1)} %bitcast.5), channel_id=1, source_target_pairs={{0,2},{1,15},{2,0},{3,5},{4,6},{5,3},{6,4},{7,9},{8,10},{9,7},{10,... | collective-permute-start | bytes 786440 | tf_op jit(solution)/shard_map/ppermute | solution.py:197
  33.0 7.8 %collective-permute-start.2 = (bf16[1024,128]{1,0:T(8,128)(2,1)S(1)}, bf16[1024,128]{1,0:T(8,128)(2,1)S(1)}, u32[]{:S(2)}, u32[]{:S(2)}) collective-permute-start(bf16[1024,128]{1,0:T(8,128)(2,1)S(1)} %collective-permute-done.1.kv_ref.refs_1_), channel_id=1, source_target_pairs={{0,14},{1,3},{2,4},{3,1},{4,2},{5,7},{6,8},{7,5},{8,6},{9,11},{10,... | collective-permute-start | bytes 786440 | tf_op jit(solution)/shard_map/ppermute | solution.py:197
  36.2 9.2 %collective-permute-start.5 = (bf16[1024,128]{1,0:T(8,128)(2,1)S(1)}, bf16[1024,128]{1,0:T(8,128)(2,1)S(1)}, u32[]{:S(2)}, u32[]{:S(2)}) collective-permute-start(bf16[1024,128]{1,0:T(8,128)(2,1)S(1)} %collective-permute-done.3.kv_ref.refs_2_), channel_id=1, source_target_pairs={{0,14},{1,3},{2,4},{3,1},{4,2},{5,7},{6,8},{7,5},{8,6},{9,11},{10,... | collective-permute-start | bytes 786440 | tf_op jit(solution)/shard_map/ppermute | solution.py:197
  40.8 9.0 %collective-permute-start.4 = (bf16[1024,128]{1,0:T(8,128)(2,1)S(1)}, bf16[1024,128]{1,0:T(8,128)(2,1)S(1)}, u32[]{:S(2)}, u32[]{:S(2)}) collective-permute-start(bf16[1024,128]{1,0:T(8,128)(2,1)S(1)} %collective-permute-done.2.kv_ref.refs_3_), channel_id=1, source_target_pairs={{0,2},{1,15},{2,0},{3,5},{4,6},{5,3},{6,4},{7,9},{8,10},{9,7},{10,... | collective-permute-start | bytes 786440 | tf_op jit(solution)/shard_map/ppermute | solution.py:197
  45.4 7.5 %collective-permute-start.7 = (bf16[1024,128]{1,0:T(8,128)(2,1)S(1)}, bf16[1024,128]{1,0:T(8,128)(2,1)S(1)}, u32[]{:S(2)}, u32[]{:S(2)}) collective-permute-start(bf16[1024,128]{1,0:T(8,128)(2,1)S(1)} %collective-permute-done.5.kv_ref.refs_4_), channel_id=1, source_target_pairs={{0,2},{1,15},{2,0},{3,5},{4,6},{5,3},{6,4},{7,9},{8,10},{9,7},{10,... | collective-permute-start | bytes 786440 | tf_op jit(solution)/shard_map/ppermute | solution.py:197
  49.8 6.2 %collective-permute-start.6 = (bf16[1024,128]{1,0:T(8,128)(2,1)S(1)}, bf16[1024,128]{1,0:T(8,128)(2,1)S(1)}, u32[]{:S(2)}, u32[]{:S(2)}) collective-permute-start(bf16[1024,128]{1,0:T(8,128)(2,1)S(1)} %collective-permute-done.4.kv_ref.refs_5_), channel_id=1, source_target_pairs={{0,14},{1,3},{2,4},{3,1},{4,2},{5,7},{6,8},{7,5},{8,6},{9,11},{10,... | collective-permute-start | bytes 786440 | tf_op jit(solution)/shard_map/ppermute | solution.py:197
  102.3 14.1 %copy-start = (bf16[1024,1024]{1,0:T(8,128)(2,1)S(1)}, bf16[1024,1024]{1,0:T(8,128)(2,1)}, u32[]{:S(2)}) copy-start(bf16[1024,1024]{1,0:T(8,128)(2,1)} %w_ref.1) | copy-start | bytes 6291460
  102.4 2.0 %collective-permute-start.8 = (f32[1024,128]{1,0:T(8,128)S(1)}, f32[1024,128]{1,0:T(8,128)S(1)}, u32[]{:S(2)}, u32[]{:S(2)}) collective-permute-start(f32[1024,128]{1,0:T(8,128)S(1)} %get-tuple-element.33), channel_id=1, source_target_pairs={{0,1},{1,0},{2,3},{3,2},{4,5},{5,4},{6,7},{7,6},{8,9},{9,8},{10,11... | collective-permute-start | bytes 1572872 | tf_op jit(solution)/shard_map/ppermute | solution.py:233
where the time goes:
time: 117 us; the launch traced here: 118 us
  Pallas kernels  73.9 us (63%)
  blocking collectives  27.3 us (23%)
  starting transfers between devices  14.1 us (12%)
  waiting for transfers between devices  1.92 us (2%)
    pallas_call x1, Pallas kernels, on_device(): call(last_kernel, acc_shape, in_specs=[vmem] * 3 + [anywhere] * len(block...  46.3 us
    pallas_call x6, Pallas kernels, on_device(): call(step_kernel, acc_shape, cost_estimate=cost(1), input_output_aliases=...  18.3 us
    all_to_all x1, blocking collectives, on_device(): mine = lax.all_to_all(packed, ('x', 'y'), 0, 0, tiled=True)  15.9 us
    ppermute x7, starting transfers between devices, exchanged(): return lax.ppermute(block, ('zh', 'zl', 'c'), pairs)  11.5 us
    all_to_all x1, blocking collectives, on_device(): heads = lax.all_to_all(attended, ('x', 'y'), 0, 0, tiled=True)  11.4 us
    pallas_call x1, Pallas kernels, on_device(): call(first_kernel, q_shape, acc_shape, cost_estimate=cost(1))  5.6 us
    ppermute x1, starting transfers between devices, on_device(): partners = lax.ppermute(mine, 'c', swap)  2.51 us
  transfers between devices with their start and end apart: 9, of which 1 were waited for; matrix products, arithmetic and copies ran while one was open for 0% of the time, Pallas kernels for 20%

commit v1 on v0

--- a/solution.py
+++ b/solution.py
@@ -16,6 +16,7 @@
 BIG = 2.0**100
 LOWEST = -1e30
 ROW_BLOCK = 512
+SHIFT_KEYS = 256
 
 NT = (((1,), (1,)), ((), ()))
 
@@ -70,15 +71,14 @@
     count = 2 * heads * rows
     q_ref[:count, :] = split_queries(q_own_ref[...].reshape(heads * rows, LANES))
     q_ref[count:, :] = split_queries(q_other_ref[...].reshape(heads * rows, LANES))
-    keys, values = keys_twice(kv_ref[...]), values_and_one(kv_ref[...])
-
-    def one(rows):
-        s = scores(q_ref, rows, keys)
-        shift = jnp.max(s, axis=1, keepdims=True)
-        p = jnp.exp2(s - shift).astype(jnp.bfloat16)
-        acc_ref[rows, :] = with_shift(jnp.dot(p, values, preferred_element_type=jnp.float32), shift)
-
-    each_row_block(q_ref, one)
+    few = keys_twice(kv_ref[:SHIFT_KEYS, :])
+
+    def begin(rows):
+        shift = jnp.max(scores(q_ref, rows, few), axis=1, keepdims=True)
+        acc_ref[rows, :] = with_shift(jnp.zeros((ROW_BLOCK, LANES), jnp.float32), shift)
+
+    each_row_block(q_ref, begin)
+    step_kernel(q_ref, kv_ref, acc_ref, acc_ref)
 
 
 def each_row_block(q_ref, step):

time: 117 us -> 118 us (level)
  starting transfers between devices: 14.1 us -> 17 us
  blocking collectives: 27.3 us -> 25.8 us
    ppermute x1, starting transfers between devices: 0.09 us -> 2.91 us  [on_device(): arrived = lax.ppermute(acc[count:], 'c', swap)]
    all_to_all x1, blocking collectives: 11.4 us -> 9.93 us  [on_device(): heads = lax.all_to_all(attended, ('x', 'y'), 0, 0, tiled=True)]
  transfers between devices with their start and end apart: 9 -> 9, of which waited for: 1 -> 1; matrix products, arithmetic and copies ran while one was open for 0% -> 0% of each run, Pallas kernels for 20% -> 19%
where the time goes in v1:
time: 118 us; the launch traced here: 117 us
  Pallas kernels  72.8 us (62%)
  blocking collectives  25.8 us (22%)
  starting transfers between devices  17 us (14%)
  waiting for transfers between devices  1.56 us (1%)
    pallas_call x1, Pallas kernels, on_device(): call(last_kernel, acc_shape, in_specs=[vmem] * 3 + [anywhere] * len(block...  46.3 us
    pallas_call x6, Pallas kernels, on_device(): call(step_kernel, acc_shape, cost_estimate=cost(1), input_output_aliases=...  18.3 us
    all_to_all x1, blocking collectives, on_device(): mine = lax.all_to_all(packed, ('x', 'y'), 0, 0, tiled=True)  15.9 us
    ppermute x7, starting transfers between devices, exchanged(): return lax.ppermute(block, ('zh', 'zl', 'c'), pairs)  11.5 us
    all_to_all x1, blocking collectives, on_device(): heads = lax.all_to_all(attended, ('x', 'y'), 0, 0, tiled=True)  9.93 us
    pallas_call x1, Pallas kernels, on_device(): call(first_kernel, q_shape, acc_shape, cost_estimate=cost(1))  4.56 us
    ppermute x1, starting transfers between devices, on_device(): arrived = lax.ppermute(acc[count:], 'c', swap)  2.91 us
    ppermute x1, starting transfers between devices, on_device(): partners = lax.ppermute(mine, 'c', swap)  2.51 us
  transfers between devices with their start and end apart: 9, of which 1 were waited for; matrix products, arithmetic and copies ran while one was open for 0% of the time, Pallas kernels for 19%

profile of v1, /device:TPU:1, one launch (start us, length us, event | category | flops | bytes accessed | tf_op | source)
XLA Modules:
  0.0 117.5 jit_solution(14111268781680307737)
XLA Ops:
  0.0 2.0 %shard_map.46 = bf16[16,96,128]{2,1,0:T(8,128)(2,1)} custom-call(bf16[64,1024]{1,0:T(8,128)(2,1)} %q_hbm.1, bf16[64,1024]{1,0:T(8,128)(2,1)} %k_hbm.1, bf16[64,1024]{1,0:T(8,128)(2,1)} %v_hbm.1), custom_call_target="tpu_custom_call" | custom-call | tf_op jit(solution)/shard_map/pallas_call | solution.py:174
  2.0 15.9 %all_to_all.10 = bf16[16,96,128]{2,1,0:T(8,128)(2,1)S(1)} all-to-all(bf16[16,96,128]{2,1,0:T(8,128)(2,1)} %shard_map.46), channel_id=1, replica_groups=mesh['x'=4,'y'=4,'zh'=2,'zl'=4,'c'=2] {'x','y'}, dimensions={0} | all-to-all | bytes 786432 | tf_op jit(solution)/shard_map/all_to_all | solution.py:182
  17.8 2.5 %collective-permute-start = (bf16[16,96,128]{2,1,0:T(8,128)(2,1)S(1)}, bf16[16,96,128]{2,1,0:T(8,128)(2,1)S(1)}, u32[]{:S(2)}, u32[]{:S(2)}) collective-permute-start(bf16[16,96,128]{2,1,0:T(8,128)(2,1)S(1)} %all_to_all.10), channel_id=1, source_target_pairs={{0,1},{1,0},{2,3},{3,2},{4,5},{5,4},{6,7},{7,6},{8,9},{9,8},{10,11... | collective-permute-start | bytes 1179656 | tf_op jit(solution)/shard_map/ppermute | solution.py:208
  20.4 5.7 %collective-permute-start.1 = (bf16[1024,128]{1,0:T(8,128)(2,1)S(1)}, bf16[1024,128]{1,0:T(8,128)(2,1)S(1)}, u32[]{:S(2)}, u32[]{:S(2)}) collective-permute-start(bf16[1024,128]{1,0:T(8,128)(2,1)S(1)} %bitcast.2), channel_id=1, source_target_pairs={{0,2},{1,15},{2,0},{3,5},{4,6},{5,3},{6,4},{7,9},{8,10},{9,7},{10,... | collective-permute-start | bytes 786440 | tf_op jit(solution)/shard_map/ppermute | solution.py:197
  26.0 0.0 collective-permute-done
  26.1 1.3 %collective-permute-start.3 = (bf16[1024,128]{1,0:T(8,128)(2,1)S(1)}, bf16[1024,128]{1,0:T(8,128)(2,1)S(1)}, u32[]{:S(2)}, u32[]{:S(2)}) collective-permute-start(bf16[1024,128]{1,0:T(8,128)(2,1)S(1)} %bitcast.5), channel_id=1, source_target_pairs={{0,2},{1,15},{2,0},{3,5},{4,6},{5,3},{6,4},{7,9},{8,10},{9,7},{10,... | collective-permute-start | bytes 786440 | tf_op jit(solution)/shard_map/ppermute | solution.py:197
  27.4 4.6 %shard_map.47 = (bf16[2048,128]{1,0:T(8,128)(2,1)S(1)}, f32[2048,128]{1,0:T(8,128)S(1)}) custom-call(bf16[16,32,128]{2,1,0:T(8,128)(2,1)S(1)} %slice.24.q_own_ref, bf16[16,32,128]{2,1,0:T(8,128)(2,1)S(1)} %slice.25.q_other_ref, bf16[1024,128]{1,0:T(8,128)(2,1)S(1)} %bitcast.3), custom_call_target="tpu_custom_call" | custom-call | flops 2147483648 | bytes 4194304 | tf_op jit(solution)/shard_map/pallas_call | solution.py:210
  32.0 0.0 collective-permute-done.1.kv_ref.refs_1_
  32.0 0.1 collective-permute-start.2
  32.1 3.1 %shard_map.48.acc_in_ref = f32[2048,128]{1,0:T(8,128)S(1)} custom-call(bf16[2048,128]{1,0:T(8,128)(2,1)S(1)} %get-tuple-element.19.q_ref, bf16[1024,128]{1,0:T(8,128)(2,1)S(1)} %collective-permute-done.1.kv_ref.refs_1_, f32[2048,128]{1,0:T(8,128)S(1)} %get-tuple-element.22.acc_in_ref), custom_call_target="tpu_custom_call", output_to_operand_aliasing={{}: (2, {})} | custom-call | flops 2147483648 | bytes 4194304 | tf_op jit(solution)/shard_map/pallas_call | solution.py:220
  35.1 0.0 collective-permute-done.3.kv_ref.refs_2_
  35.1 1.5 %collective-permute-start.5 = (bf16[1024,128]{1,0:T(8,128)(2,1)S(1)}, bf16[1024,128]{1,0:T(8,128)(2,1)S(1)}, u32[]{:S(2)}, u32[]{:S(2)}) collective-permute-start(bf16[1024,128]{1,0:T(8,128)(2,1)S(1)} %collective-permute-done.3.kv_ref.refs_2_), channel_id=1, source_target_pairs={{0,14},{1,3},{2,4},{3,1},{4,2},{5,7},{6,8},{7,5},{8,6},{9,11},{10,... | collective-permute-start | bytes 786440 | tf_op jit(solution)/shard_map/ppermute | solution.py:197
  36.7 3.1 %shard_map.49.acc_in_ref = f32[2048,128]{1,0:T(8,128)S(1)} custom-call(bf16[2048,128]{1,0:T(8,128)(2,1)S(1)} %get-tuple-element.19.q_ref, bf16[1024,128]{1,0:T(8,128)(2,1)S(1)} %collective-permute-done.3.kv_ref.refs_2_, f32[2048,128]{1,0:T(8,128)S(1)} %shard_map.48.acc_in_ref), custom_call_target="tpu_custom_call", output_to_operand_aliasing={{}: (2, {})} | custom-call | flops 2147483648 | bytes 4194304 | tf_op jit(solution)/shard_map/pallas_call | solution.py:220
  39.8 0.0 collective-permute-done.2.kv_ref.refs_3_
  39.8 1.5 %collective-permute-start.4 = (bf16[1024,128]{1,0:T(8,128)(2,1)S(1)}, bf16[1024,128]{1,0:T(8,128)(2,1)S(1)}, u32[]{:S(2)}, u32[]{:S(2)}) collective-permute-start(bf16[1024,128]{1,0:T(8,128)(2,1)S(1)} %collective-permute-done.2.kv_ref.refs_3_), channel_id=1, source_target_pairs={{0,2},{1,15},{2,0},{3,5},{4,6},{5,3},{6,4},{7,9},{8,10},{9,7},{10,... | collective-permute-start | bytes 786440 | tf_op jit(solution)/shard_map/ppermute | solution.py:197
  41.3 3.0 %shard_map.50.acc_in_ref = f32[2048,128]{1,0:T(8,128)S(1)} custom-call(bf16[2048,128]{1,0:T(8,128)(2,1)S(1)} %get-tuple-element.19.q_ref, bf16[1024,128]{1,0:T(8,128)(2,1)S(1)} %collective-permute-done.2.kv_ref.refs_3_, f32[2048,128]{1,0:T(8,128)S(1)} %shard_map.49.acc_in_ref), custom_call_target="tpu_custom_call", output_to_operand_aliasing={{}: (2, {})} | custom-call | flops 2147483648 | bytes 4194304 | tf_op jit(solution)/shard_map/pallas_call | solution.py:220
  44.4 0.0 collective-permute-done.5.kv_ref.refs_4_
  44.4 1.3 %collective-permute-start.7 = (bf16[1024,128]{1,0:T(8,128)(2,1)S(1)}, bf16[1024,128]{1,0:T(8,128)(2,1)S(1)}, u32[]{:S(2)}, u32[]{:S(2)}) collective-permute-start(bf16[1024,128]{1,0:T(8,128)(2,1)S(1)} %collective-permute-done.5.kv_ref.refs_4_), channel_id=1, source_target_pairs={{0,2},{1,15},{2,0},{3,5},{4,6},{5,3},{6,4},{7,9},{8,10},{9,7},{10,... | collective-permute-start | bytes 786440 | tf_op jit(solution)/shard_map/ppermute | solution.py:197
  45.7 3.0 %shard_map.51.acc_in_ref = f32[2048,128]{1,0:T(8,128)S(1)} custom-call(bf16[2048,128]{1,0:T(8,128)(2,1)S(1)} %get-tuple-element.19.q_ref, bf16[1024,128]{1,0:T(8,128)(2,1)S(1)} %collective-permute-done.5.kv_ref.refs_4_, f32[2048,128]{1,0:T(8,128)S(1)} %shard_map.50.acc_in_ref), custom_call_target="tpu_custom_call", output_to_operand_aliasing={{}: (2, {})} | custom-call | flops 2147483648 | bytes 4194304 | tf_op jit(solution)/shard_map/pallas_call | solution.py:220
  48.7 0.0 collective-permute-done.4.kv_ref.refs_5_
  48.7 0.1 collective-permute-start.6
  48.8 3.0 %shard_map.52.acc_in_ref = f32[2048,128]{1,0:T(8,128)S(1)} custom-call(bf16[2048,128]{1,0:T(8,128)(2,1)S(1)} %get-tuple-element.19.q_ref, bf16[1024,128]{1,0:T(8,128)(2,1)S(1)} %collective-permute-done.4.kv_ref.refs_5_, f32[2048,128]{1,0:T(8,128)S(1)} %shard_map.51.acc_in_ref), custom_call_target="tpu_custom_call", output_to_operand_aliasing={{}: (2, {})} | custom-call | flops 2147483648 | bytes 4194304 | tf_op jit(solution)/shard_map/pallas_call | solution.py:220
  51.9 0.0 collective-permute-done.7.kv_ref.refs_6_
  51.9 3.0 %shard_map.53.acc_in_ref = f32[2048,128]{1,0:T(8,128)S(1)} custom-call(bf16[2048,128]{1,0:T(8,128)(2,1)S(1)} %get-tuple-element.19.q_ref, bf16[1024,128]{1,0:T(8,128)(2,1)S(1)} %collective-permute-done.7.kv_ref.refs_6_, f32[2048,128]{1,0:T(8,128)S(1)} %shard_map.52.acc_in_ref), custom_call_target="tpu_custom_call", output_to_operand_aliasing={{}: (2, {})} | custom-call | flops 2147483648 | bytes 4194304 | tf_op jit(solution)/shard_map/pallas_call | solution.py:220
  55.0 0.0 collective-permute-done.6.kv_ref.refs_7_
  55.0 46.3 %shard_map.54 = f32[2048,128]{1,0:T(8,128)S(1)} custom-call(bf16[2048,128]{1,0:T(8,128)(2,1)S(1)} %get-tuple-element.19.q_ref, bf16[1024,128]{1,0:T(8,128)(2,1)S(1)} %collective-permute-done.6.kv_ref.refs_7_, f32[2048,128]{1,0:T(8,128)S(1)} %shard_map.53.acc_in_ref, bf16[1024,128]{1,0:T(8,128)(2,1)S(1)} %bitcast.4, ...), custom_call_target="tpu_custom_call", output_to_operand_aliasing={{}: (2, {})} | custom-call | flops 2147483648 | bytes 4194304 | tf_op jit(solution)/shard_map/pallas_call | solution.py:224
  101.3 0.0 copy-start
  101.3 0.1 fusion
  101.4 2.9 %collective-permute-start.8 = (f32[1024,128]{1,0:T(8,128)S(1)}, f32[1024,128]{1,0:T(8,128)S(1)}, u32[]{:S(2)}, u32[]{:S(2)}) collective-permute-start(f32[1024,128]{1,0:T(8,128)S(1)} %get-tuple-element.33), channel_id=1, source_target_pairs={{0,1},{1,0},{2,3},{3,2},{4,5},{5,4},{6,7},{7,6},{8,9},{9,8},{10,11... | collective-permute-start | bytes 1572872 | tf_op jit(solution)/shard_map/ppermute | solution.py:233
  104.3 1.5 %collective-permute-done.8.other_ref = f32[1024,128]{1,0:T(8,128)S(1)} collective-permute-done((f32[1024,128]{1,0:T(8,128)S(1)}, f32[1024,128]{1,0:T(8,128)S(1)}, u32[]{:S(2)}, u32[]{:S(2)}) %collective-permute-start.8) | collective-permute-done | bytes 524320 | tf_op jit(solution)/shard_map/ppermute | solution.py:233
  105.8 0.6 shard_map.55
  106.4 9.9 %all_to_all.11.heads_ref = bf16[16,32,128]{2,1,0:T(8,128)(2,1)S(1)} all-to-all(bf16[16,32,128]{2,1,0:T(8,128)(2,1)S(1)} %shard_map.55), channel_id=1, replica_groups=mesh['x'=4,'y'=4,'zh'=2,'zl'=4,'c'=2] {'x','y'}, dimensions={0} | all-to-all | bytes 262144 | tf_op jit(solution)/shard_map/all_to_all | solution.py:236
  116.3 0.0 copy-done
  116.3 1.2 shard_map.56
  (4 shorter events, 0.1 us)
Async XLA Ops:
  17.8 8.2 %collective-permute-start = (bf16[16,96,128]{2,1,0:T(8,128)(2,1)S(1)}, bf16[16,96,128]{2,1,0:T(8,128)(2,1)S(1)}, u32[]{:S(2)}, u32[]{:S(2)}) collective-permute-start(bf16[16,96,128]{2,1,0:T(8,128)(2,1)S(1)} %all_to_all.10), channel_id=1, source_target_pairs={{0,1},{1,0},{2,3},{3,2},{4,5},{5,4},{6,7},{7,6},{8,9},{9,8},{10,11... | collective-permute-start | bytes 1179656 | tf_op jit(solution)/shard_map/ppermute | solution.py:208
  20.4 11.6 %collective-permute-start.1 = (bf16[1024,128]{1,0:T(8,128)(2,1)S(1)}, bf16[1024,128]{1,0:T(8,128)(2,1)S(1)}, u32[]{:S(2)}, u32[]{:S(2)}) collective-permute-start(bf16[1024,128]{1,0:T(8,128)(2,1)S(1)} %bitcast.2), channel_id=1, source_target_pairs={{0,2},{1,15},{2,0},{3,5},{4,6},{5,3},{6,4},{7,9},{8,10},{9,7},{10,... | collective-permute-start | bytes 786440 | tf_op jit(solution)/shard_map/ppermute | solution.py:197
  26.1 9.1 %collective-permute-start.3 = (bf16[1024,128]{1,0:T(8,128)(2,1)S(1)}, bf16[1024,128]{1,0:T(8,128)(2,1)S(1)}, u32[]{:S(2)}, u32[]{:S(2)}) collective-permute-start(bf16[1024,128]{1,0:T(8,128)(2,1)S(1)} %bitcast.5), channel_id=1, source_target_pairs={{0,2},{1,15},{2,0},{3,5},{4,6},{5,3},{6,4},{7,9},{8,10},{9,7},{10,... | collective-permute-start | bytes 786440 | tf_op jit(solution)/shard_map/ppermute | solution.py:197
  32.0 7.8 %collective-permute-start.2 = (bf16[1024,128]{1,0:T(8,128)(2,1)S(1)}, bf16[1024,128]{1,0:T(8,128)(2,1)S(1)}, u32[]{:S(2)}, u32[]{:S(2)}) collective-permute-start(bf16[1024,128]{1,0:T(8,128)(2,1)S(1)} %collective-permute-done.1.kv_ref.refs_1_), channel_id=1, source_target_pairs={{0,14},{1,3},{2,4},{3,1},{4,2},{5,7},{6,8},{7,5},{8,6},{9,11},{10,... | collective-permute-start | bytes 786440 | tf_op jit(solution)/shard_map/ppermute | solution.py:197
  35.1 9.2 %collective-permute-start.5 = (bf16[1024,128]{1,0:T(8,128)(2,1)S(1)}, bf16[1024,128]{1,0:T(8,128)(2,1)S(1)}, u32[]{:S(2)}, u32[]{:S(2)}) collective-permute-start(bf16[1024,128]{1,0:T(8,128)(2,1)S(1)} %collective-permute-done.3.kv_ref.refs_2_), channel_id=1, source_target_pairs={{0,14},{1,3},{2,4},{3,1},{4,2},{5,7},{6,8},{7,5},{8,6},{9,11},{10,... | collective-permute-start | bytes 786440 | tf_op jit(solution)/shard_map/ppermute | solution.py:197
  39.8 9.0 %collective-permute-start.4 = (bf16[1024,128]{1,0:T(8,128)(2,1)S(1)}, bf16[1024,128]{1,0:T(8,128)(2,1)S(1)}, u32[]{:S(2)}, u32[]{:S(2)}) collective-permute-start(bf16[1024,128]{1,0:T(8,128)(2,1)S(1)} %collective-permute-done.2.kv_ref.refs_3_), channel_id=1, source_target_pairs={{0,2},{1,15},{2,0},{3,5},{4,6},{5,3},{6,4},{7,9},{8,10},{9,7},{10,... | collective-permute-start | bytes 786440 | tf_op jit(solution)/shard_map/ppermute | solution.py:197
  44.4 7.5 %collective-permute-start.7 = (bf16[1024,128]{1,0:T(8,128)(2,1)S(1)}, bf16[1024,128]{1,0:T(8,128)(2,1)S(1)}, u32[]{:S(2)}, u32[]{:S(2)}) collective-permute-start(bf16[1024,128]{1,0:T(8,128)(2,1)S(1)} %collective-permute-done.5.kv_ref.refs_4_), channel_id=1, source_target_pairs={{0,2},{1,15},{2,0},{3,5},{4,6},{5,3},{6,4},{7,9},{8,10},{9,7},{10,... | collective-permute-start | bytes 786440 | tf_op jit(solution)/shard_map/ppermute | solution.py:197
  48.7 6.2 %collective-permute-start.6 = (bf16[1024,128]{1,0:T(8,128)(2,1)S(1)}, bf16[1024,128]{1,0:T(8,128)(2,1)S(1)}, u32[]{:S(2)}, u32[]{:S(2)}) collective-permute-start(bf16[1024,128]{1,0:T(8,128)(2,1)S(1)} %collective-permute-done.4.kv_ref.refs_5_), channel_id=1, source_target_pairs={{0,14},{1,3},{2,4},{3,1},{4,2},{5,7},{6,8},{7,5},{8,6},{9,11},{10,... | collective-permute-start | bytes 786440 | tf_op jit(solution)/shard_map/ppermute | solution.py:197
  101.3 15.0 %copy-start = (bf16[1024,1024]{1,0:T(8,128)(2,1)S(1)}, bf16[1024,1024]{1,0:T(8,128)(2,1)}, u32[]{:S(2)}) copy-start(bf16[1024,1024]{1,0:T(8,128)(2,1)} %w_ref.1) | copy-start | bytes 6291460
  101.4 4.4 %collective-permute-start.8 = (f32[1024,128]{1,0:T(8,128)S(1)}, f32[1024,128]{1,0:T(8,128)S(1)}, u32[]{:S(2)}, u32[]{:S(2)}) collective-permute-start(f32[1024,128]{1,0:T(8,128)S(1)} %get-tuple-element.33), channel_id=1, source_target_pairs={{0,1},{1,0},{2,3},{3,2},{4,5},{5,4},{6,7},{7,6},{8,9},{9,8},{10,11... | collective-permute-start | bytes 1572872 | tf_op jit(solution)/shard_map/ppermute | solution.py:233

commit v2 on v1

--- a/solution.py
+++ b/solution.py
@@ -15,8 +15,9 @@
 LOG2E = 1.4426950408889634
 BIG = 2.0**100
 LOWEST = -1e30
-ROW_BLOCK = 512
-SHIFT_KEYS = 256
+ROW_BLOCK = 1024
+REDO_BLOCK = 256
+SHIFT_KEYS = 128
 
 NT = (((1,), (1,)), ((), ()))
 
@@ -81,12 +82,12 @@
     step_kernel(q_ref, kv_ref, acc_ref, acc_ref)
 
 
-def each_row_block(q_ref, step):
+def each_row_block(q_ref, step, size=ROW_BLOCK):
     def body(i, carry):
-        step(pl.ds(pl.multiple_of(i * ROW_BLOCK, ROW_BLOCK), ROW_BLOCK))
+        step(pl.ds(pl.multiple_of(i * size, size), size))
         return carry
 
-    lax.fori_loop(0, q_ref.shape[0] // ROW_BLOCK, body, 0)
+    lax.fori_loop(0, q_ref.shape[0] // size, body, 0)
 
 
 def step_kernel(q_ref, kv_ref, acc_in_ref, acc_ref):
@@ -128,7 +129,7 @@
         contrib = jnp.dot(p, values, preferred_element_type=jnp.float32)
         acc_ref[rows, :] = with_shift(acc * jnp.exp2(before - highest) + contrib, highest)
 
-    each_row_block(q_ref, one)
+    each_row_block(q_ref, one, REDO_BLOCK)
 
 
 def merge_kernel(own_ref, other_ref, out_ref):

time: 118 us -> 123 us (1.042)
  Pallas kernels: 72.8 us -> 78.5 us
    pallas_call x1, Pallas kernels: 46.3 us -> 54.5 us  [on_device(): call(last_kernel, acc_shape, in_specs=[vmem] * 3 + [anywhere] * len(block...]
    pallas_call x6, Pallas kernels: 18.3 us -> 16.4 us  [on_device(): call(step_kernel, acc_shape, cost_estimate=cost(1), input_output_aliases=...]
  transfers between devices with their start and end apart: 9 -> 9, of which waited for: 1 -> 2; matrix products, arithmetic and copies ran while one was open for 0% -> 0% of each run, Pallas kernels for 19% -> 16%
where the time goes in v2:
time: 123 us
  Pallas kernels  78.5 us (64%)
  blocking collectives  25.8 us (21%)
  starting transfers between devices  16.9 us (14%)
  waiting for transfers between devices  1.73 us (1%)
    pallas_call x1, Pallas kernels, on_device(): call(last_kernel, acc_shape, in_specs=[vmem] * 3 + [anywhere] * len(block...  54.5 us
    pallas_call x6, Pallas kernels, on_device(): call(step_kernel, acc_shape, cost_estimate=cost(1), input_output_aliases=...  16.4 us
    all_to_all x1, blocking collectives, on_device(): mine = lax.all_to_all(packed, ('x', 'y'), 0, 0, tiled=True)  15.9 us
    ppermute x7, starting transfers between devices, exchanged(): return lax.ppermute(block, ('zh', 'zl', 'c'), pairs)  11.7 us
    all_to_all x1, blocking collectives, on_device(): heads = lax.all_to_all(attended, ('x', 'y'), 0, 0, tiled=True)  9.93 us
    pallas_call x1, Pallas kernels, on_device(): call(first_kernel, q_shape, acc_shape, cost_estimate=cost(1))  3.77 us
    ppermute x1, starting transfers between devices, on_device(): arrived = lax.ppermute(acc[count:], 'c', swap)  2.67 us
    ppermute x1, starting transfers between devices, on_device(): partners = lax.ppermute(mine, 'c', swap)  2.51 us
  transfers between devices with their start and end apart: 9, of which 2 were waited for; matrix products, arithmetic and copies ran while one was open for 0% of the time, Pallas kernels for 16%

profile of v2, /device:TPU:1, one launch (start us, length us, event | category | flops | bytes accessed | tf_op | source)
XLA Modules:
  0.0 123.2 jit_solution(2761857172713088336)
XLA Ops:
  0.0 2.0 %shard_map.46 = bf16[16,96,128]{2,1,0:T(8,128)(2,1)} custom-call(bf16[64,1024]{1,0:T(8,128)(2,1)} %q_hbm.1, bf16[64,1024]{1,0:T(8,128)(2,1)} %k_hbm.1, bf16[64,1024]{1,0:T(8,128)(2,1)} %v_hbm.1), custom_call_target="tpu_custom_call" | custom-call | tf_op jit(solution)/shard_map/pallas_call | solution.py:175
  2.0 15.9 %all_to_all.10 = bf16[16,96,128]{2,1,0:T(8,128)(2,1)S(1)} all-to-all(bf16[16,96,128]{2,1,0:T(8,128)(2,1)} %shard_map.46), channel_id=1, replica_groups=mesh['x'=4,'y'=4,'zh'=2,'zl'=4,'c'=2] {'x','y'}, dimensions={0} | all-to-all | bytes 786432 | tf_op jit(solution)/shard_map/all_to_all | solution.py:183
  17.8 2.5 %collective-permute-start = (bf16[16,96,128]{2,1,0:T(8,128)(2,1)S(1)}, bf16[16,96,128]{2,1,0:T(8,128)(2,1)S(1)}, u32[]{:S(2)}, u32[]{:S(2)}) collective-permute-start(bf16[16,96,128]{2,1,0:T(8,128)(2,1)S(1)} %all_to_all.10), channel_id=1, source_target_pairs={{0,1},{1,0},{2,3},{3,2},{4,5},{5,4},{6,7},{7,6},{8,9},{9,8},{10,11... | collective-permute-start | bytes 1179656 | tf_op jit(solution)/shard_map/ppermute | solution.py:209
  20.4 5.7 %collective-permute-start.1 = (bf16[1024,128]{1,0:T(8,128)(2,1)S(1)}, bf16[1024,128]{1,0:T(8,128)(2,1)S(1)}, u32[]{:S(2)}, u32[]{:S(2)}) collective-permute-start(bf16[1024,128]{1,0:T(8,128)(2,1)S(1)} %bitcast.2), channel_id=1, source_target_pairs={{0,2},{1,15},{2,0},{3,5},{4,6},{5,3},{6,4},{7,9},{8,10},{9,7},{10,... | collective-permute-start | bytes 786440 | tf_op jit(solution)/shard_map/ppermute | solution.py:198
  26.0 0.0 collective-permute-done
  26.1 1.3 %collective-permute-start.3 = (bf16[1024,128]{1,0:T(8,128)(2,1)S(1)}, bf16[1024,128]{1,0:T(8,128)(2,1)S(1)}, u32[]{:S(2)}, u32[]{:S(2)}) collective-permute-start(bf16[1024,128]{1,0:T(8,128)(2,1)S(1)} %bitcast.5), channel_id=1, source_target_pairs={{0,2},{1,15},{2,0},{3,5},{4,6},{5,3},{6,4},{7,9},{8,10},{9,7},{10,... | collective-permute-start | bytes 786440 | tf_op jit(solution)/shard_map/ppermute | solution.py:198
  27.4 3.8 %shard_map.47 = (bf16[2048,128]{1,0:T(8,128)(2,1)S(1)}, f32[2048,128]{1,0:T(8,128)S(1)}) custom-call(bf16[16,32,128]{2,1,0:T(8,128)(2,1)S(1)} %slice.24.q_own_ref, bf16[16,32,128]{2,1,0:T(8,128)(2,1)S(1)} %slice.25.q_other_ref, bf16[1024,128]{1,0:T(8,128)(2,1)S(1)} %bitcast.3), custom_call_target="tpu_custom_call" | custom-call | flops 2147483648 | bytes 4194304 | tf_op jit(solution)/shard_map/pallas_call | solution.py:211
  31.2 0.0 collective-permute-done.1.kv_ref.refs_1_
  31.2 0.1 collective-permute-start.2
  31.3 2.7 %shard_map.48.acc_in_ref = f32[2048,128]{1,0:T(8,128)S(1)} custom-call(bf16[2048,128]{1,0:T(8,128)(2,1)S(1)} %get-tuple-element.19.q_ref, bf16[1024,128]{1,0:T(8,128)(2,1)S(1)} %collective-permute-done.1.kv_ref.refs_1_, f32[2048,128]{1,0:T(8,128)S(1)} %get-tuple-element.22.acc_in_ref), custom_call_target="tpu_custom_call", output_to_operand_aliasing={{}: (2, {})} | custom-call | flops 2147483648 | bytes 4194304 | tf_op jit(solution)/shard_map/pallas_call | solution.py:221
  34.0 0.0 collective-permute-done.3.kv_ref.refs_2_
  34.0 1.5 %collective-permute-start.5 = (bf16[1024,128]{1,0:T(8,128)(2,1)S(1)}, bf16[1024,128]{1,0:T(8,128)(2,1)S(1)}, u32[]{:S(2)}, u32[]{:S(2)}) collective-permute-start(bf16[1024,128]{1,0:T(8,128)(2,1)S(1)} %collective-permute-done.3.kv_ref.refs_2_), channel_id=1, source_target_pairs={{0,14},{1,3},{2,4},{3,1},{4,2},{5,7},{6,8},{7,5},{8,6},{9,11},{10,... | collective-permute-start | bytes 786440 | tf_op jit(solution)/shard_map/ppermute | solution.py:198
  35.6 2.7 %shard_map.49.acc_in_ref = f32[2048,128]{1,0:T(8,128)S(1)} custom-call(bf16[2048,128]{1,0:T(8,128)(2,1)S(1)} %get-tuple-element.19.q_ref, bf16[1024,128]{1,0:T(8,128)(2,1)S(1)} %collective-permute-done.3.kv_ref.refs_2_, f32[2048,128]{1,0:T(8,128)S(1)} %shard_map.48.acc_in_ref), custom_call_target="tpu_custom_call", output_to_operand_aliasing={{}: (2, {})} | custom-call | flops 2147483648 | bytes 4194304 | tf_op jit(solution)/shard_map/pallas_call | solution.py:221
  38.3 0.0 collective-permute-done.2.kv_ref.refs_3_
  38.3 1.6 %collective-permute-start.4 = (bf16[1024,128]{1,0:T(8,128)(2,1)S(1)}, bf16[1024,128]{1,0:T(8,128)(2,1)S(1)}, u32[]{:S(2)}, u32[]{:S(2)}) collective-permute-start(bf16[1024,128]{1,0:T(8,128)(2,1)S(1)} %collective-permute-done.2.kv_ref.refs_3_), channel_id=1, source_target_pairs={{0,2},{1,15},{2,0},{3,5},{4,6},{5,3},{6,4},{7,9},{8,10},{9,7},{10,... | collective-permute-start | bytes 786440 | tf_op jit(solution)/shard_map/ppermute | solution.py:198
  39.9 2.7 %shard_map.50.acc_in_ref = f32[2048,128]{1,0:T(8,128)S(1)} custom-call(bf16[2048,128]{1,0:T(8,128)(2,1)S(1)} %get-tuple-element.19.q_ref, bf16[1024,128]{1,0:T(8,128)(2,1)S(1)} %collective-permute-done.2.kv_ref.refs_3_, f32[2048,128]{1,0:T(8,128)S(1)} %shard_map.49.acc_in_ref), custom_call_target="tpu_custom_call", output_to_operand_aliasing={{}: (2, {})} | custom-call | flops 2147483648 | bytes 4194304 | tf_op jit(solution)/shard_map/pallas_call | solution.py:221
  42.6 0.0 collective-permute-done.5.kv_ref.refs_4_
  42.7 1.3 %collective-permute-start.7 = (bf16[1024,128]{1,0:T(8,128)(2,1)S(1)}, bf16[1024,128]{1,0:T(8,128)(2,1)S(1)}, u32[]{:S(2)}, u32[]{:S(2)}) collective-permute-start(bf16[1024,128]{1,0:T(8,128)(2,1)S(1)} %collective-permute-done.5.kv_ref.refs_4_), channel_id=1, source_target_pairs={{0,2},{1,15},{2,0},{3,5},{4,6},{5,3},{6,4},{7,9},{8,10},{9,7},{10,... | collective-permute-start | bytes 786440 | tf_op jit(solution)/shard_map/ppermute | solution.py:198
  44.0 2.7 %shard_map.51.acc_in_ref = f32[2048,128]{1,0:T(8,128)S(1)} custom-call(bf16[2048,128]{1,0:T(8,128)(2,1)S(1)} %get-tuple-element.19.q_ref, bf16[1024,128]{1,0:T(8,128)(2,1)S(1)} %collective-permute-done.5.kv_ref.refs_4_, f32[2048,128]{1,0:T(8,128)S(1)} %shard_map.50.acc_in_ref), custom_call_target="tpu_custom_call", output_to_operand_aliasing={{}: (2, {})} | custom-call | flops 2147483648 | bytes 4194304 | tf_op jit(solution)/shard_map/pallas_call | solution.py:221
  46.7 0.0 collective-permute-done.4.kv_ref.refs_5_
  46.7 0.3 collective-permute-start.6
  47.0 2.7 %shard_map.52.acc_in_ref = f32[2048,128]{1,0:T(8,128)S(1)} custom-call(bf16[2048,128]{1,0:T(8,128)(2,1)S(1)} %get-tuple-element.19.q_ref, bf16[1024,128]{1,0:T(8,128)(2,1)S(1)} %collective-permute-done.4.kv_ref.refs_5_, f32[2048,128]{1,0:T(8,128)S(1)} %shard_map.51.acc_in_ref), custom_call_target="tpu_custom_call", output_to_operand_aliasing={{}: (2, {})} | custom-call | flops 2147483648 | bytes 4194304 | tf_op jit(solution)/shard_map/pallas_call | solution.py:221
  49.7 0.0 collective-permute-done.7.kv_ref.refs_6_
  49.8 2.7 %shard_map.53.acc_in_ref = f32[2048,128]{1,0:T(8,128)S(1)} custom-call(bf16[2048,128]{1,0:T(8,128)(2,1)S(1)} %get-tuple-element.19.q_ref, bf16[1024,128]{1,0:T(8,128)(2,1)S(1)} %collective-permute-done.7.kv_ref.refs_6_, f32[2048,128]{1,0:T(8,128)S(1)} %shard_map.52.acc_in_ref), custom_call_target="tpu_custom_call", output_to_operand_aliasing={{}: (2, {})} | custom-call | flops 2147483648 | bytes 4194304 | tf_op jit(solution)/shard_map/pallas_call | solution.py:221
  52.5 0.2 collective-permute-done.6.kv_ref.refs_7_
  52.7 54.5 %shard_map.54 = f32[2048,128]{1,0:T(8,128)S(1)} custom-call(bf16[2048,128]{1,0:T(8,128)(2,1)S(1)} %get-tuple-element.19.q_ref, bf16[1024,128]{1,0:T(8,128)(2,1)S(1)} %collective-permute-done.6.kv_ref.refs_7_, f32[2048,128]{1,0:T(8,128)S(1)} %shard_map.53.acc_in_ref, bf16[1024,128]{1,0:T(8,128)(2,1)S(1)} %bitcast.4, ...), custom_call_target="tpu_custom_call", output_to_operand_aliasing={{}: (2, {})} | custom-call | flops 2147483648 | bytes 4194304 | tf_op jit(solution)/shard_map/pallas_call | solution.py:225
  107.2 0.0 copy-start
  107.2 0.1 fusion
  107.3 2.7 %collective-permute-start.8 = (f32[1024,128]{1,0:T(8,128)S(1)}, f32[1024,128]{1,0:T(8,128)S(1)}, u32[]{:S(2)}, u32[]{:S(2)}) collective-permute-start(f32[1024,128]{1,0:T(8,128)S(1)} %get-tuple-element.33), channel_id=1, source_target_pairs={{0,1},{1,0},{2,3},{3,2},{4,5},{5,4},{6,7},{7,6},{8,9},{9,8},{10,11... | collective-permute-start | bytes 1572872 | tf_op jit(solution)/shard_map/ppermute | solution.py:234
  110.0 1.5 %collective-permute-done.8.other_ref = f32[1024,128]{1,0:T(8,128)S(1)} collective-permute-done((f32[1024,128]{1,0:T(8,128)S(1)}, f32[1024,128]{1,0:T(8,128)S(1)}, u32[]{:S(2)}, u32[]{:S(2)}) %collective-permute-start.8) | collective-permute-done | bytes 524320 | tf_op jit(solution)/shard_map/ppermute | solution.py:234
  111.5 0.6 shard_map.55
  112.1 9.9 %all_to_all.11.heads_ref = bf16[16,32,128]{2,1,0:T(8,128)(2,1)S(1)} all-to-all(bf16[16,32,128]{2,1,0:T(8,128)(2,1)S(1)} %shard_map.55), channel_id=1, replica_groups=mesh['x'=4,'y'=4,'zh'=2,'zl'=4,'c'=2] {'x','y'}, dimensions={0} | all-to-all | bytes 262144 | tf_op jit(solution)/shard_map/all_to_all | solution.py:237
  122.0 0.0 copy-done
  122.0 1.2 shard_map.56
  (4 shorter events, 0.1 us)
Async XLA Ops:
  17.8 8.2 %collective-permute-start = (bf16[16,96,128]{2,1,0:T(8,128)(2,1)S(1)}, bf16[16,96,128]{2,1,0:T(8,128)(2,1)S(1)}, u32[]{:S(2)}, u32[]{:S(2)}) collective-permute-start(bf16[16,96,128]{2,1,0:T(8,128)(2,1)S(1)} %all_to_all.10), channel_id=1, source_target_pairs={{0,1},{1,0},{2,3},{3,2},{4,5},{5,4},{6,7},{7,6},{8,9},{9,8},{10,11... | collective-permute-start | bytes 1179656 | tf_op jit(solution)/shard_map/ppermute | solution.py:209
  20.4 10.8 %collective-permute-start.1 = (bf16[1024,128]{1,0:T(8,128)(2,1)S(1)}, bf16[1024,128]{1,0:T(8,128)(2,1)S(1)}, u32[]{:S(2)}, u32[]{:S(2)}) collective-permute-start(bf16[1024,128]{1,0:T(8,128)(2,1)S(1)} %bitcast.2), channel_id=1, source_target_pairs={{0,2},{1,15},{2,0},{3,5},{4,6},{5,3},{6,4},{7,9},{8,10},{9,7},{10,... | collective-permute-start | bytes 786440 | tf_op jit(solution)/shard_map/ppermute | solution.py:198
  26.1 8.0 %collective-permute-start.3 = (bf16[1024,128]{1,0:T(8,128)(2,1)S(1)}, bf16[1024,128]{1,0:T(8,128)(2,1)S(1)}, u32[]{:S(2)}, u32[]{:S(2)}) collective-permute-start(bf16[1024,128]{1,0:T(8,128)(2,1)S(1)} %bitcast.5), channel_id=1, source_target_pairs={{0,2},{1,15},{2,0},{3,5},{4,6},{5,3},{6,4},{7,9},{8,10},{9,7},{10,... | collective-permute-start | bytes 786440 | tf_op jit(solution)/shard_map/ppermute | solution.py:198
  31.2 7.1 %collective-permute-start.2 = (bf16[1024,128]{1,0:T(8,128)(2,1)S(1)}, bf16[1024,128]{1,0:T(8,128)(2,1)S(1)}, u32[]{:S(2)}, u32[]{:S(2)}) collective-permute-start(bf16[1024,128]{1,0:T(8,128)(2,1)S(1)} %collective-permute-done.1.kv_ref.refs_1_), channel_id=1, source_target_pairs={{0,14},{1,3},{2,4},{3,1},{4,2},{5,7},{6,8},{7,5},{8,6},{9,11},{10,... | collective-permute-start | bytes 786440 | tf_op jit(solution)/shard_map/ppermute | solution.py:198
  34.0 8.6 %collective-permute-start.5 = (bf16[1024,128]{1,0:T(8,128)(2,1)S(1)}, bf16[1024,128]{1,0:T(8,128)(2,1)S(1)}, u32[]{:S(2)}, u32[]{:S(2)}) collective-permute-start(bf16[1024,128]{1,0:T(8,128)(2,1)S(1)} %collective-permute-done.3.kv_ref.refs_2_), channel_id=1, source_target_pairs={{0,14},{1,3},{2,4},{3,1},{4,2},{5,7},{6,8},{7,5},{8,6},{9,11},{10,... | collective-permute-start | bytes 786440 | tf_op jit(solution)/shard_map/ppermute | solution.py:198
  38.3 8.4 %collective-permute-start.4 = (bf16[1024,128]{1,0:T(8,128)(2,1)S(1)}, bf16[1024,128]{1,0:T(8,128)(2,1)S(1)}, u32[]{:S(2)}, u32[]{:S(2)}) collective-permute-start(bf16[1024,128]{1,0:T(8,128)(2,1)S(1)} %collective-permute-done.2.kv_ref.refs_3_), channel_id=1, source_target_pairs={{0,2},{1,15},{2,0},{3,5},{4,6},{5,3},{6,4},{7,9},{8,10},{9,7},{10,... | collective-permute-start | bytes 786440 | tf_op jit(solution)/shard_map/ppermute | solution.py:198
  42.7 7.1 %collective-permute-start.7 = (bf16[1024,128]{1,0:T(8,128)(2,1)S(1)}, bf16[1024,128]{1,0:T(8,128)(2,1)S(1)}, u32[]{:S(2)}, u32[]{:S(2)}) collective-permute-start(bf16[1024,128]{1,0:T(8,128)(2,1)S(1)} %collective-permute-done.5.kv_ref.refs_4_), channel_id=1, source_target_pairs={{0,2},{1,15},{2,0},{3,5},{4,6},{5,3},{6,4},{7,9},{8,10},{9,7},{10,... | collective-permute-start | bytes 786440 | tf_op jit(solution)/shard_map/ppermute | solution.py:198
  46.7 6.0 %collective-permute-start.6 = (bf16[1024,128]{1,0:T(8,128)(2,1)S(1)}, bf16[1024,128]{1,0:T(8,128)(2,1)S(1)}, u32[]{:S(2)}, u32[]{:S(2)}) collective-permute-start(bf16[1024,128]{1,0:T(8,128)(2,1)S(1)} %collective-permute-done.4.kv_ref.refs_5_), channel_id=1, source_target_pairs={{0,14},{1,3},{2,4},{3,1},{4,2},{5,7},{6,8},{7,5},{8,6},{9,11},{10,... | collective-permute-start | bytes 786440 | tf_op jit(solution)/shard_map/ppermute | solution.py:198
  107.2 14.8 %copy-start = (bf16[1024,1024]{1,0:T(8,128)(2,1)S(1)}, bf16[1024,1024]{1,0:T(8,128)(2,1)}, u32[]{:S(2)}) copy-start(bf16[1024,1024]{1,0:T(8,128)(2,1)} %w_ref.1) | copy-start | bytes 6291460
  107.3 4.2 %collective-permute-start.8 = (f32[1024,128]{1,0:T(8,128)S(1)}, f32[1024,128]{1,0:T(8,128)S(1)}, u32[]{:S(2)}, u32[]{:S(2)}) collective-permute-start(f32[1024,128]{1,0:T(8,128)S(1)} %get-tuple-element.33), channel_id=1, source_target_pairs={{0,1},{1,0},{2,3},{3,2},{4,5},{5,4},{6,7},{7,6},{8,9},{9,8},{10,11... | collective-permute-start | bytes 1572872 | tf_op jit(solution)/shard_map/ppermute | solution.py:234

commit v3 on v2

--- a/solution.py
+++ b/solution.py
@@ -15,7 +15,7 @@
 LOG2E = 1.4426950408889634
 BIG = 2.0**100
 LOWEST = -1e30
-ROW_BLOCK = 1024
+ROW_BLOCK = 2048
 REDO_BLOCK = 256
 SHIFT_KEYS = 128
 

time: 123 us -> 125 us (1.016)
  no operation moved by 1% of the time
where the time goes in v3:
time: 125 us
  Pallas kernels  78.9 us (63%)
  blocking collectives  25.8 us (21%)
  starting transfers between devices  17.8 us (14%)
  waiting for transfers between devices  1.78 us (1%)
    pallas_call x1, Pallas kernels, on_device(): call(last_kernel, acc_shape, in_specs=[vmem] * 3 + [anywhere] * len(block...  55 us
    pallas_call x6, Pallas kernels, on_device(): call(step_kernel, acc_shape, cost_estimate=cost(1), input_output_aliases=...  17.5 us
    all_to_all x1, blocking collectives, on_device(): mine = lax.all_to_all(packed, ('x', 'y'), 0, 0, tiled=True)  15.9 us
    ppermute x7, starting transfers between devices, exchanged(): return lax.ppermute(block, ('zh', 'zl', 'c'), pairs)  11.9 us
    all_to_all x1, blocking collectives, on_device(): heads = lax.all_to_all(attended, ('x', 'y'), 0, 0, tiled=True)  9.93 us
    ppermute x1, starting transfers between devices, on_device(): arrived = lax.ppermute(acc[count:], 'c', swap)  3.35 us
    pallas_call x1, Pallas kernels, on_device(): call(first_kernel, q_shape, acc_shape, cost_estimate=cost(1))  2.81 us
    ppermute x1, starting transfers between devices, on_device(): partners = lax.ppermute(mine, 'c', swap)  2.51 us
  transfers between devices with their start and end apart: 9, of which 2 were waited for; matrix products, arithmetic and copies ran while one was open for 0% of the time, Pallas kernels for 16%

profile of v3, /device:TPU:1, one launch (start us, length us, event | category | flops | bytes accessed | tf_op | source)
XLA Modules:
  0.0 124.6 jit_solution(2864418499988925160)
XLA Ops:
  0.0 2.0 %shard_map.46 = bf16[16,96,128]{2,1,0:T(8,128)(2,1)} custom-call(bf16[64,1024]{1,0:T(8,128)(2,1)} %q_hbm.1, bf16[64,1024]{1,0:T(8,128)(2,1)} %k_hbm.1, bf16[64,1024]{1,0:T(8,128)(2,1)} %v_hbm.1), custom_call_target="tpu_custom_call" | custom-call | tf_op jit(solution)/shard_map/pallas_call | solution.py:175
  2.0 15.9 %all_to_all.10 = bf16[16,96,128]{2,1,0:T(8,128)(2,1)S(1)} all-to-all(bf16[16,96,128]{2,1,0:T(8,128)(2,1)} %shard_map.46), channel_id=1, replica_groups=mesh['x'=4,'y'=4,'zh'=2,'zl'=4,'c'=2] {'x','y'}, dimensions={0} | all-to-all | bytes 786432 | tf_op jit(solution)/shard_map/all_to_all | solution.py:183
  17.8 2.5 %collective-permute-start = (bf16[16,96,128]{2,1,0:T(8,128)(2,1)S(1)}, bf16[16,96,128]{2,1,0:T(8,128)(2,1)S(1)}, u32[]{:S(2)}, u32[]{:S(2)}) collective-permute-start(bf16[16,96,128]{2,1,0:T(8,128)(2,1)S(1)} %all_to_all.10), channel_id=1, source_target_pairs={{0,1},{1,0},{2,3},{3,2},{4,5},{5,4},{6,7},{7,6},{8,9},{9,8},{10,11... | collective-permute-start | bytes 1179656 | tf_op jit(solution)/shard_map/ppermute | solution.py:209
  20.4 5.7 %collective-permute-start.1 = (bf16[1024,128]{1,0:T(8,128)(2,1)S(1)}, bf16[1024,128]{1,0:T(8,128)(2,1)S(1)}, u32[]{:S(2)}, u32[]{:S(2)}) collective-permute-start(bf16[1024,128]{1,0:T(8,128)(2,1)S(1)} %bitcast.2), channel_id=1, source_target_pairs={{0,2},{1,15},{2,0},{3,5},{4,6},{5,3},{6,4},{7,9},{8,10},{9,7},{10,... | collective-permute-start | bytes 786440 | tf_op jit(solution)/shard_map/ppermute | solution.py:198
  26.0 0.0 collective-permute-done
  26.1 1.3 %collective-permute-start.3 = (bf16[1024,128]{1,0:T(8,128)(2,1)S(1)}, bf16[1024,128]{1,0:T(8,128)(2,1)S(1)}, u32[]{:S(2)}, u32[]{:S(2)}) collective-permute-start(bf16[1024,128]{1,0:T(8,128)(2,1)S(1)} %bitcast.5), channel_id=1, source_target_pairs={{0,2},{1,15},{2,0},{3,5},{4,6},{5,3},{6,4},{7,9},{8,10},{9,7},{10,... | collective-permute-start | bytes 786440 | tf_op jit(solution)/shard_map/ppermute | solution.py:198
  27.4 2.8 %shard_map.47 = (bf16[2048,128]{1,0:T(8,128)(2,1)S(1)}, f32[2048,128]{1,0:T(8,128)S(1)}) custom-call(bf16[16,32,128]{2,1,0:T(8,128)(2,1)S(1)} %slice.24.q_own_ref, bf16[16,32,128]{2,1,0:T(8,128)(2,1)S(1)} %slice.25.q_other_ref, bf16[1024,128]{1,0:T(8,128)(2,1)S(1)} %bitcast.3), custom_call_target="tpu_custom_call" | custom-call | flops 2147483648 | bytes 4194304 | tf_op jit(solution)/shard_map/pallas_call | solution.py:211
  30.2 0.0 collective-permute-done.1.kv_ref.refs_1_
  30.2 0.1 collective-permute-start.2
  30.3 2.9 %shard_map.48.acc_in_ref = f32[2048,128]{1,0:T(8,128)S(1)} custom-call(bf16[2048,128]{1,0:T(8,128)(2,1)S(1)} %get-tuple-element.19.q_ref, bf16[1024,128]{1,0:T(8,128)(2,1)S(1)} %collective-permute-done.1.kv_ref.refs_1_, f32[2048,128]{1,0:T(8,128)S(1)} %get-tuple-element.22.acc_in_ref), custom_call_target="tpu_custom_call", output_to_operand_aliasing={{}: (2, {})} | custom-call | flops 2147483648 | bytes 4194304 | tf_op jit(solution)/shard_map/pallas_call | solution.py:221
  33.2 0.0 collective-permute-done.3.kv_ref.refs_2_
  33.3 1.5 %collective-permute-start.5 = (bf16[1024,128]{1,0:T(8,128)(2,1)S(1)}, bf16[1024,128]{1,0:T(8,128)(2,1)S(1)}, u32[]{:S(2)}, u32[]{:S(2)}) collective-permute-start(bf16[1024,128]{1,0:T(8,128)(2,1)S(1)} %collective-permute-done.3.kv_ref.refs_2_), channel_id=1, source_target_pairs={{0,14},{1,3},{2,4},{3,1},{4,2},{5,7},{6,8},{7,5},{8,6},{9,11},{10,... | collective-permute-start | bytes 786440 | tf_op jit(solution)/shard_map/ppermute | solution.py:198
  34.8 2.9 %shard_map.49.acc_in_ref = f32[2048,128]{1,0:T(8,128)S(1)} custom-call(bf16[2048,128]{1,0:T(8,128)(2,1)S(1)} %get-tuple-element.19.q_ref, bf16[1024,128]{1,0:T(8,128)(2,1)S(1)} %collective-permute-done.3.kv_ref.refs_2_, f32[2048,128]{1,0:T(8,128)S(1)} %shard_map.48.acc_in_ref), custom_call_target="tpu_custom_call", output_to_operand_aliasing={{}: (2, {})} | custom-call | flops 2147483648 | bytes 4194304 | tf_op jit(solution)/shard_map/pallas_call | solution.py:221
  37.7 0.0 collective-permute-done.2.kv_ref.refs_3_
  37.7 2.4 %collective-permute-start.4 = (bf16[1024,128]{1,0:T(8,128)(2,1)S(1)}, bf16[1024,128]{1,0:T(8,128)(2,1)S(1)}, u32[]{:S(2)}, u32[]{:S(2)}) collective-permute-start(bf16[1024,128]{1,0:T(8,128)(2,1)S(1)} %collective-permute-done.2.kv_ref.refs_3_), channel_id=1, source_target_pairs={{0,2},{1,15},{2,0},{3,5},{4,6},{5,3},{6,4},{7,9},{8,10},{9,7},{10,... | collective-permute-start | bytes 786440 | tf_op jit(solution)/shard_map/ppermute | solution.py:198
  40.1 2.9 %shard_map.50.acc_in_ref = f32[2048,128]{1,0:T(8,128)S(1)} custom-call(bf16[2048,128]{1,0:T(8,128)(2,1)S(1)} %get-tuple-element.19.q_ref, bf16[1024,128]{1,0:T(8,128)(2,1)S(1)} %collective-permute-done.2.kv_ref.refs_3_, f32[2048,128]{1,0:T(8,128)S(1)} %shard_map.49.acc_in_ref), custom_call_target="tpu_custom_call", output_to_operand_aliasing={{}: (2, {})} | custom-call | flops 2147483648 | bytes 4194304 | tf_op jit(solution)/shard_map/pallas_call | solution.py:221
  43.1 0.0 collective-permute-done.5.kv_ref.refs_4_
  43.1 0.6 collective-permute-start.7
  43.7 2.9 %shard_map.51.acc_in_ref = f32[2048,128]{1,0:T(8,128)S(1)} custom-call(bf16[2048,128]{1,0:T(8,128)(2,1)S(1)} %get-tuple-element.19.q_ref, bf16[1024,128]{1,0:T(8,128)(2,1)S(1)} %collective-permute-done.5.kv_ref.refs_4_, f32[2048,128]{1,0:T(8,128)S(1)} %shard_map.50.acc_in_ref), custom_call_target="tpu_custom_call", output_to_operand_aliasing={{}: (2, {})} | custom-call | flops 2147483648 | bytes 4194304 | tf_op jit(solution)/shard_map/pallas_call | solution.py:221
  46.6 0.0 collective-permute-done.4.kv_ref.refs_5_
  46.6 0.3 collective-permute-start.6
  46.9 2.9 %shard_map.52.acc_in_ref = f32[2048,128]{1,0:T(8,128)S(1)} custom-call(bf16[2048,128]{1,0:T(8,128)(2,1)S(1)} %get-tuple-element.19.q_ref, bf16[1024,128]{1,0:T(8,128)(2,1)S(1)} %collective-permute-done.4.kv_ref.refs_5_, f32[2048,128]{1,0:T(8,128)S(1)} %shard_map.51.acc_in_ref), custom_call_target="tpu_custom_call", output_to_operand_aliasing={{}: (2, {})} | custom-call | flops 2147483648 | bytes 4194304 | tf_op jit(solution)/shard_map/pallas_call | solution.py:221
  49.8 0.0 collective-permute-done.7.kv_ref.refs_6_
  49.9 2.9 %shard_map.53.acc_in_ref = f32[2048,128]{1,0:T(8,128)S(1)} custom-call(bf16[2048,128]{1,0:T(8,128)(2,1)S(1)} %get-tuple-element.19.q_ref, bf16[1024,128]{1,0:T(8,128)(2,1)S(1)} %collective-permute-done.7.kv_ref.refs_6_, f32[2048,128]{1,0:T(8,128)S(1)} %shard_map.52.acc_in_ref), custom_call_target="tpu_custom_call", output_to_operand_aliasing={{}: (2, {})} | custom-call | flops 2147483648 | bytes 4194304 | tf_op jit(solution)/shard_map/pallas_call | solution.py:221
  52.8 0.2 collective-permute-done.6.kv_ref.refs_7_
  53.0 55.0 %shard_map.54 = f32[2048,128]{1,0:T(8,128)S(1)} custom-call(bf16[2048,128]{1,0:T(8,128)(2,1)S(1)} %get-tuple-element.19.q_ref, bf16[1024,128]{1,0:T(8,128)(2,1)S(1)} %collective-permute-done.6.kv_ref.refs_7_, f32[2048,128]{1,0:T(8,128)S(1)} %shard_map.53.acc_in_ref, bf16[1024,128]{1,0:T(8,128)(2,1)S(1)} %bitcast.4, ...), custom_call_target="tpu_custom_call", output_to_operand_aliasing={{}: (2, {})} | custom-call | flops 2147483648 | bytes 4194304 | tf_op jit(solution)/shard_map/pallas_call | solution.py:225
  108.0 0.0 copy-start
  108.0 0.1 fusion
  108.0 3.4 %collective-permute-start.8 = (f32[1024,128]{1,0:T(8,128)S(1)}, f32[1024,128]{1,0:T(8,128)S(1)}, u32[]{:S(2)}, u32[]{:S(2)}) collective-permute-start(f32[1024,128]{1,0:T(8,128)S(1)} %get-tuple-element.33), channel_id=1, source_target_pairs={{0,1},{1,0},{2,3},{3,2},{4,5},{5,4},{6,7},{7,6},{8,9},{9,8},{10,11... | collective-permute-start | bytes 1572872 | tf_op jit(solution)/shard_map/ppermute | solution.py:234
  111.4 1.5 %collective-permute-done.8.other_ref = f32[1024,128]{1,0:T(8,128)S(1)} collective-permute-done((f32[1024,128]{1,0:T(8,128)S(1)}, f32[1024,128]{1,0:T(8,128)S(1)}, u32[]{:S(2)}, u32[]{:S(2)}) %collective-permute-start.8) | collective-permute-done | bytes 524320 | tf_op jit(solution)/shard_map/ppermute | solution.py:234
  112.9 0.6 shard_map.55
  113.5 9.9 %all_to_all.11.heads_ref = bf16[16,32,128]{2,1,0:T(8,128)(2,1)S(1)} all-to-all(bf16[16,32,128]{2,1,0:T(8,128)(2,1)S(1)} %shard_map.55), channel_id=1, replica_groups=mesh['x'=4,'y'=4,'zh'=2,'zl'=4,'c'=2] {'x','y'}, dimensions={0} | all-to-all | bytes 262144 | tf_op jit(solution)/shard_map/all_to_all | solution.py:237
  123.4 0.0 copy-done
  123.4 1.2 shard_map.56
  (4 shorter events, 0.1 us)
Async XLA Ops:
  17.8 8.2 %collective-permute-start = (bf16[16,96,128]{2,1,0:T(8,128)(2,1)S(1)}, bf16[16,96,128]{2,1,0:T(8,128)(2,1)S(1)}, u32[]{:S(2)}, u32[]{:S(2)}) collective-permute-start(bf16[16,96,128]{2,1,0:T(8,128)(2,1)S(1)} %all_to_all.10), channel_id=1, source_target_pairs={{0,1},{1,0},{2,3},{3,2},{4,5},{5,4},{6,7},{7,6},{8,9},{9,8},{10,11... | collective-permute-start | bytes 1179656 | tf_op jit(solution)/shard_map/ppermute | solution.py:209
  20.4 9.8 %collective-permute-start.1 = (bf16[1024,128]{1,0:T(8,128)(2,1)S(1)}, bf16[1024,128]{1,0:T(8,128)(2,1)S(1)}, u32[]{:S(2)}, u32[]{:S(2)}) collective-permute-start(bf16[1024,128]{1,0:T(8,128)(2,1)S(1)} %bitcast.2), channel_id=1, source_target_pairs={{0,2},{1,15},{2,0},{3,5},{4,6},{5,3},{6,4},{7,9},{8,10},{9,7},{10,... | collective-permute-start | bytes 786440 | tf_op jit(solution)/shard_map/ppermute | solution.py:198
  26.1 7.2 %collective-permute-start.3 = (bf16[1024,128]{1,0:T(8,128)(2,1)S(1)}, bf16[1024,128]{1,0:T(8,128)(2,1)S(1)}, u32[]{:S(2)}, u32[]{:S(2)}) collective-permute-start(bf16[1024,128]{1,0:T(8,128)(2,1)S(1)} %bitcast.5), channel_id=1, source_target_pairs={{0,2},{1,15},{2,0},{3,5},{4,6},{5,3},{6,4},{7,9},{8,10},{9,7},{10,... | collective-permute-start | bytes 786440 | tf_op jit(solution)/shard_map/ppermute | solution.py:198
  30.2 7.5 %collective-permute-start.2 = (bf16[1024,128]{1,0:T(8,128)(2,1)S(1)}, bf16[1024,128]{1,0:T(8,128)(2,1)S(1)}, u32[]{:S(2)}, u32[]{:S(2)}) collective-permute-start(bf16[1024,128]{1,0:T(8,128)(2,1)S(1)} %collective-permute-done.1.kv_ref.refs_1_), channel_id=1, source_target_pairs={{0,14},{1,3},{2,4},{3,1},{4,2},{5,7},{6,8},{7,5},{8,6},{9,11},{10,... | collective-permute-start | bytes 786440 | tf_op jit(solution)/shard_map/ppermute | solution.py:198
  33.3 9.8 %collective-permute-start.5 = (bf16[1024,128]{1,0:T(8,128)(2,1)S(1)}, bf16[1024,128]{1,0:T(8,128)(2,1)S(1)}, u32[]{:S(2)}, u32[]{:S(2)}) collective-permute-start(bf16[1024,128]{1,0:T(8,128)(2,1)S(1)} %collective-permute-done.3.kv_ref.refs_2_), channel_id=1, source_target_pairs={{0,14},{1,3},{2,4},{3,1},{4,2},{5,7},{6,8},{7,5},{8,6},{9,11},{10,... | collective-permute-start | bytes 786440 | tf_op jit(solution)/shard_map/ppermute | solution.py:198
  37.7 8.9 %collective-permute-start.4 = (bf16[1024,128]{1,0:T(8,128)(2,1)S(1)}, bf16[1024,128]{1,0:T(8,128)(2,1)S(1)}, u32[]{:S(2)}, u32[]{:S(2)}) collective-permute-start(bf16[1024,128]{1,0:T(8,128)(2,1)S(1)} %collective-permute-done.2.kv_ref.refs_3_), channel_id=1, source_target_pairs={{0,2},{1,15},{2,0},{3,5},{4,6},{5,3},{6,4},{7,9},{8,10},{9,7},{10,... | collective-permute-start | bytes 786440 | tf_op jit(solution)/shard_map/ppermute | solution.py:198
  43.1 6.8 %collective-permute-start.7 = (bf16[1024,128]{1,0:T(8,128)(2,1)S(1)}, bf16[1024,128]{1,0:T(8,128)(2,1)S(1)}, u32[]{:S(2)}, u32[]{:S(2)}) collective-permute-start(bf16[1024,128]{1,0:T(8,128)(2,1)S(1)} %collective-permute-done.5.kv_ref.refs_4_), channel_id=1, source_target_pairs={{0,2},{1,15},{2,0},{3,5},{4,6},{5,3},{6,4},{7,9},{8,10},{9,7},{10,... | collective-permute-start | bytes 786440 | tf_op jit(solution)/shard_map/ppermute | solution.py:198
  46.6 6.4 %collective-permute-start.6 = (bf16[1024,128]{1,0:T(8,128)(2,1)S(1)}, bf16[1024,128]{1,0:T(8,128)(2,1)S(1)}, u32[]{:S(2)}, u32[]{:S(2)}) collective-permute-start(bf16[1024,128]{1,0:T(8,128)(2,1)S(1)} %collective-permute-done.4.kv_ref.refs_5_), channel_id=1, source_target_pairs={{0,14},{1,3},{2,4},{3,1},{4,2},{5,7},{6,8},{7,5},{8,6},{9,11},{10,... | collective-permute-start | bytes 786440 | tf_op jit(solution)/shard_map/ppermute | solution.py:198
  108.0 15.5 %copy-start = (bf16[1024,1024]{1,0:T(8,128)(2,1)S(1)}, bf16[1024,1024]{1,0:T(8,128)(2,1)}, u32[]{:S(2)}) copy-start(bf16[1024,1024]{1,0:T(8,128)(2,1)} %w_ref.1) | copy-start | bytes 6291460
  108.0 4.9 %collective-permute-start.8 = (f32[1024,128]{1,0:T(8,128)S(1)}, f32[1024,128]{1,0:T(8,128)S(1)}, u32[]{:S(2)}, u32[]{:S(2)}) collective-permute-start(f32[1024,128]{1,0:T(8,128)S(1)} %get-tuple-element.33), channel_id=1, source_target_pairs={{0,1},{1,0},{2,3},{3,2},{4,5},{5,4},{6,7},{7,6},{8,9},{9,8},{10,11... | collective-permute-start | bytes 1572872 | tf_op jit(solution)/shard_map/ppermute | solution.py:234

commit v4 on v2

--- a/solution.py
+++ b/solution.py
@@ -110,11 +110,16 @@
     @pl.when(jnp.logical_not(fine))
     def _():
         acc_ref[...] = with_shift(jnp.zeros_like(acc_ref), LOWEST)
-        for other_kv_ref in kv_refs:
-            copy = pltpu.make_async_copy(other_kv_ref, kv_buf, sem)
+        for n, other_kv_ref in enumerate(kv_refs):
+            copy = pltpu.make_async_copy(other_kv_ref, kv_buf.at[n], sem)
             copy.start()
             copy.wait()
-            redo_block(q_ref, kv_buf, acc_ref)
+
+        def redo(n, carry):
+            redo_block(q_ref, kv_buf.at[n], acc_ref)
+            return carry
+
+        lax.fori_loop(0, len(kv_refs), redo, 0)
 
 
 def redo_block(q_ref, kv_ref, acc_ref):
@@ -227,7 +232,7 @@
         acc_shape,
         in_specs=[vmem] * 3 + [anywhere] * len(blocks),
         out_specs=vmem,
-        scratch_shapes=[pltpu.VMEM((count, LANES), bf16), pltpu.SemaphoreType.DMA],
+        scratch_shapes=[pltpu.VMEM((len(blocks), count, LANES), bf16), pltpu.SemaphoreType.DMA],
         cost_estimate=cost(1),
         input_output_aliases={2: 0},
     )(q_all, chains[0], acc, *blocks)

time: 123 us -> 123 us (level)
  no operation moved by 1% of the time
where the time goes in v4:
time: 123 us
  Pallas kernels  78.5 us (64%)
  blocking collectives  25.8 us (21%)
  starting transfers between devices  16.9 us (14%)
  waiting for transfers between devices  1.73 us (1%)
    pallas_call x1, Pallas kernels, on_device(): call(last_kernel, acc_shape, in_specs=[vmem] * 3 + [anywhere] * len(block...  54.6 us
    pallas_call x6, Pallas kernels, on_device(): call(step_kernel, acc_shape, cost_estimate=cost(1), input_output_aliases=...  16.4 us
    all_to_all x1, blocking collectives, on_device(): mine = lax.all_to_all(packed, ('x', 'y'), 0, 0, tiled=True)  15.9 us
    ppermute x7, starting transfers between devices, exchanged(): return lax.ppermute(block, ('zh', 'zl', 'c'), pairs)  11.7 us
    all_to_all x1, blocking collectives, on_device(): heads = lax.all_to_all(attended, ('x', 'y'), 0, 0, tiled=True)  9.93 us
    pallas_call x1, Pallas kernels, on_device(): call(first_kernel, q_shape, acc_shape, cost_estimate=cost(1))  3.77 us
    ppermute x1, starting transfers between devices, on_device(): arrived = lax.ppermute(acc[count:], 'c', swap)  2.67 us
    ppermute x1, starting transfers between devices, on_device(): partners = lax.ppermute(mine, 'c', swap)  2.51 us
  transfers between devices with their start and end apart: 9, of which 2 were waited for; matrix products, arithmetic and copies ran while one was open for 0% of the time, Pallas kernels for 16%

profile of v4, /device:TPU:1, one launch (start us, length us, event | category | flops | bytes accessed | tf_op | source)
XLA Modules:
  0.0 123.2 jit_solution(15354047131715702729)
XLA Ops:
  0.0 2.0 %shard_map.46 = bf16[16,96,128]{2,1,0:T(8,128)(2,1)} custom-call(bf16[64,1024]{1,0:T(8,128)(2,1)} %q_hbm.1, bf16[64,1024]{1,0:T(8,128)(2,1)} %k_hbm.1, bf16[64,1024]{1,0:T(8,128)(2,1)} %v_hbm.1), custom_call_target="tpu_custom_call" | custom-call | tf_op jit(solution)/shard_map/pallas_call | solution.py:180
  2.0 15.9 %all_to_all.10 = bf16[16,96,128]{2,1,0:T(8,128)(2,1)S(1)} all-to-all(bf16[16,96,128]{2,1,0:T(8,128)(2,1)} %shard_map.46), channel_id=1, replica_groups=mesh['x'=4,'y'=4,'zh'=2,'zl'=4,'c'=2] {'x','y'}, dimensions={0} | all-to-all | bytes 786432 | tf_op jit(solution)/shard_map/all_to_all | solution.py:188
  17.8 2.5 %collective-permute-start = (bf16[16,96,128]{2,1,0:T(8,128)(2,1)S(1)}, bf16[16,96,128]{2,1,0:T(8,128)(2,1)S(1)}, u32[]{:S(2)}, u32[]{:S(2)}) collective-permute-start(bf16[16,96,128]{2,1,0:T(8,128)(2,1)S(1)} %all_to_all.10), channel_id=1, source_target_pairs={{0,1},{1,0},{2,3},{3,2},{4,5},{5,4},{6,7},{7,6},{8,9},{9,8},{10,11... | collective-permute-start | bytes 1179656 | tf_op jit(solution)/shard_map/ppermute | solution.py:214
  20.4 5.7 %collective-permute-start.1 = (bf16[1024,128]{1,0:T(8,128)(2,1)S(1)}, bf16[1024,128]{1,0:T(8,128)(2,1)S(1)}, u32[]{:S(2)}, u32[]{:S(2)}) collective-permute-start(bf16[1024,128]{1,0:T(8,128)(2,1)S(1)} %bitcast.2), channel_id=1, source_target_pairs={{0,2},{1,15},{2,0},{3,5},{4,6},{5,3},{6,4},{7,9},{8,10},{9,7},{10,... | collective-permute-start | bytes 786440 | tf_op jit(solution)/shard_map/ppermute | solution.py:203
  26.0 0.0 collective-permute-done
  26.1 1.3 %collective-permute-start.3 = (bf16[1024,128]{1,0:T(8,128)(2,1)S(1)}, bf16[1024,128]{1,0:T(8,128)(2,1)S(1)}, u32[]{:S(2)}, u32[]{:S(2)}) collective-permute-start(bf16[1024,128]{1,0:T(8,128)(2,1)S(1)} %bitcast.5), channel_id=1, source_target_pairs={{0,2},{1,15},{2,0},{3,5},{4,6},{5,3},{6,4},{7,9},{8,10},{9,7},{10,... | collective-permute-start | bytes 786440 | tf_op jit(solution)/shard_map/ppermute | solution.py:203
  27.4 3.8 %shard_map.47 = (bf16[2048,128]{1,0:T(8,128)(2,1)S(1)}, f32[2048,128]{1,0:T(8,128)S(1)}) custom-call(bf16[16,32,128]{2,1,0:T(8,128)(2,1)S(1)} %slice.24.q_own_ref, bf16[16,32,128]{2,1,0:T(8,128)(2,1)S(1)} %slice.25.q_other_ref, bf16[1024,128]{1,0:T(8,128)(2,1)S(1)} %bitcast.3), custom_call_target="tpu_custom_call" | custom-call | flops 2147483648 | bytes 4194304 | tf_op jit(solution)/shard_map/pallas_call | solution.py:216
  31.2 0.0 collective-permute-done.1.kv_ref.refs_1_
  31.2 0.1 collective-permute-start.2
  31.3 2.7 %shard_map.48.acc_in_ref = f32[2048,128]{1,0:T(8,128)S(1)} custom-call(bf16[2048,128]{1,0:T(8,128)(2,1)S(1)} %get-tuple-element.19.q_ref, bf16[1024,128]{1,0:T(8,128)(2,1)S(1)} %collective-permute-done.1.kv_ref.refs_1_, f32[2048,128]{1,0:T(8,128)S(1)} %get-tuple-element.22.acc_in_ref), custom_call_target="tpu_custom_call", output_to_operand_aliasing={{}: (2, {})} | custom-call | flops 2147483648 | bytes 4194304 | tf_op jit(solution)/shard_map/pallas_call | solution.py:226
  34.0 0.0 collective-permute-done.3.kv_ref.refs_2_
  34.0 1.5 %collective-permute-start.5 = (bf16[1024,128]{1,0:T(8,128)(2,1)S(1)}, bf16[1024,128]{1,0:T(8,128)(2,1)S(1)}, u32[]{:S(2)}, u32[]{:S(2)}) collective-permute-start(bf16[1024,128]{1,0:T(8,128)(2,1)S(1)} %collective-permute-done.3.kv_ref.refs_2_), channel_id=1, source_target_pairs={{0,14},{1,3},{2,4},{3,1},{4,2},{5,7},{6,8},{7,5},{8,6},{9,11},{10,... | collective-permute-start | bytes 786440 | tf_op jit(solution)/shard_map/ppermute | solution.py:203
  35.6 2.7 %shard_map.49.acc_in_ref = f32[2048,128]{1,0:T(8,128)S(1)} custom-call(bf16[2048,128]{1,0:T(8,128)(2,1)S(1)} %get-tuple-element.19.q_ref, bf16[1024,128]{1,0:T(8,128)(2,1)S(1)} %collective-permute-done.3.kv_ref.refs_2_, f32[2048,128]{1,0:T(8,128)S(1)} %shard_map.48.acc_in_ref), custom_call_target="tpu_custom_call", output_to_operand_aliasing={{}: (2, {})} | custom-call | flops 2147483648 | bytes 4194304 | tf_op jit(solution)/shard_map/pallas_call | solution.py:226
  38.3 0.0 collective-permute-done.2.kv_ref.refs_3_
  38.3 1.6 %collective-permute-start.4 = (bf16[1024,128]{1,0:T(8,128)(2,1)S(1)}, bf16[1024,128]{1,0:T(8,128)(2,1)S(1)}, u32[]{:S(2)}, u32[]{:S(2)}) collective-permute-start(bf16[1024,128]{1,0:T(8,128)(2,1)S(1)} %collective-permute-done.2.kv_ref.refs_3_), channel_id=1, source_target_pairs={{0,2},{1,15},{2,0},{3,5},{4,6},{5,3},{6,4},{7,9},{8,10},{9,7},{10,... | collective-permute-start | bytes 786440 | tf_op jit(solution)/shard_map/ppermute | solution.py:203
  39.9 2.7 %shard_map.50.acc_in_ref = f32[2048,128]{1,0:T(8,128)S(1)} custom-call(bf16[2048,128]{1,0:T(8,128)(2,1)S(1)} %get-tuple-element.19.q_ref, bf16[1024,128]{1,0:T(8,128)(2,1)S(1)} %collective-permute-done.2.kv_ref.refs_3_, f32[2048,128]{1,0:T(8,128)S(1)} %shard_map.49.acc_in_ref), custom_call_target="tpu_custom_call", output_to_operand_aliasing={{}: (2, {})} | custom-call | flops 2147483648 | bytes 4194304 | tf_op jit(solution)/shard_map/pallas_call | solution.py:226
  42.6 0.0 collective-permute-done.5.kv_ref.refs_4_
  42.7 1.3 %collective-permute-start.7 = (bf16[1024,128]{1,0:T(8,128)(2,1)S(1)}, bf16[1024,128]{1,0:T(8,128)(2,1)S(1)}, u32[]{:S(2)}, u32[]{:S(2)}) collective-permute-start(bf16[1024,128]{1,0:T(8,128)(2,1)S(1)} %collective-permute-done.5.kv_ref.refs_4_), channel_id=1, source_target_pairs={{0,2},{1,15},{2,0},{3,5},{4,6},{5,3},{6,4},{7,9},{8,10},{9,7},{10,... | collective-permute-start | bytes 786440 | tf_op jit(solution)/shard_map/ppermute | solution.py:203
  44.0 2.7 %shard_map.51.acc_in_ref = f32[2048,128]{1,0:T(8,128)S(1)} custom-call(bf16[2048,128]{1,0:T(8,128)(2,1)S(1)} %get-tuple-element.19.q_ref, bf16[1024,128]{1,0:T(8,128)(2,1)S(1)} %collective-permute-done.5.kv_ref.refs_4_, f32[2048,128]{1,0:T(8,128)S(1)} %shard_map.50.acc_in_ref), custom_call_target="tpu_custom_call", output_to_operand_aliasing={{}: (2, {})} | custom-call | flops 2147483648 | bytes 4194304 | tf_op jit(solution)/shard_map/pallas_call | solution.py:226
  46.7 0.0 collective-permute-done.4.kv_ref.refs_5_
  46.7 0.3 collective-permute-start.6
  47.0 2.7 %shard_map.52.acc_in_ref = f32[2048,128]{1,0:T(8,128)S(1)} custom-call(bf16[2048,128]{1,0:T(8,128)(2,1)S(1)} %get-tuple-element.19.q_ref, bf16[1024,128]{1,0:T(8,128)(2,1)S(1)} %collective-permute-done.4.kv_ref.refs_5_, f32[2048,128]{1,0:T(8,128)S(1)} %shard_map.51.acc_in_ref), custom_call_target="tpu_custom_call", output_to_operand_aliasing={{}: (2, {})} | custom-call | flops 2147483648 | bytes 4194304 | tf_op jit(solution)/shard_map/pallas_call | solution.py:226
  49.7 0.0 collective-permute-done.7.kv_ref.refs_6_
  49.8 2.7 %shard_map.53.acc_in_ref = f32[2048,128]{1,0:T(8,128)S(1)} custom-call(bf16[2048,128]{1,0:T(8,128)(2,1)S(1)} %get-tuple-element.19.q_ref, bf16[1024,128]{1,0:T(8,128)(2,1)S(1)} %collective-permute-done.7.kv_ref.refs_6_, f32[2048,128]{1,0:T(8,128)S(1)} %shard_map.52.acc_in_ref), custom_call_target="tpu_custom_call", output_to_operand_aliasing={{}: (2, {})} | custom-call | flops 2147483648 | bytes 4194304 | tf_op jit(solution)/shard_map/pallas_call | solution.py:226
  52.5 0.2 collective-permute-done.6.kv_ref.refs_7_
  52.7 54.6 %shard_map.54 = f32[2048,128]{1,0:T(8,128)S(1)} custom-call(bf16[2048,128]{1,0:T(8,128)(2,1)S(1)} %get-tuple-element.19.q_ref, bf16[1024,128]{1,0:T(8,128)(2,1)S(1)} %collective-permute-done.6.kv_ref.refs_7_, f32[2048,128]{1,0:T(8,128)S(1)} %shard_map.53.acc_in_ref, bf16[1024,128]{1,0:T(8,128)(2,1)S(1)} %bitcast.4, ...), custom_call_target="tpu_custom_call", output_to_operand_aliasing={{}: (2, {})} | custom-call | flops 2147483648 | bytes 4194304 | tf_op jit(solution)/shard_map/pallas_call | solution.py:230
  107.3 0.0 copy-start
  107.3 0.1 fusion
  107.3 2.7 %collective-permute-start.8 = (f32[1024,128]{1,0:T(8,128)S(1)}, f32[1024,128]{1,0:T(8,128)S(1)}, u32[]{:S(2)}, u32[]{:S(2)}) collective-permute-start(f32[1024,128]{1,0:T(8,128)S(1)} %get-tuple-element.33), channel_id=1, source_target_pairs={{0,1},{1,0},{2,3},{3,2},{4,5},{5,4},{6,7},{7,6},{8,9},{9,8},{10,11... | collective-permute-start | bytes 1572872 | tf_op jit(solution)/shard_map/ppermute | solution.py:239
  110.0 1.5 %collective-permute-done.8.other_ref = f32[1024,128]{1,0:T(8,128)S(1)} collective-permute-done((f32[1024,128]{1,0:T(8,128)S(1)}, f32[1024,128]{1,0:T(8,128)S(1)}, u32[]{:S(2)}, u32[]{:S(2)}) %collective-permute-start.8) | collective-permute-done | bytes 524320 | tf_op jit(solution)/shard_map/ppermute | solution.py:239
  111.6 0.6 shard_map.55
  112.1 9.9 %all_to_all.11.heads_ref = bf16[16,32,128]{2,1,0:T(8,128)(2,1)S(1)} all-to-all(bf16[16,32,128]{2,1,0:T(8,128)(2,1)S(1)} %shard_map.55), channel_id=1, replica_groups=mesh['x'=4,'y'=4,'zh'=2,'zl'=4,'c'=2] {'x','y'}, dimensions={0} | all-to-all | bytes 262144 | tf_op jit(solution)/shard_map/all_to_all | solution.py:242
  122.0 0.0 copy-done
  122.0 1.2 shard_map.56
  (4 shorter events, 0.1 us)
Async XLA Ops:
  17.8 8.2 %collective-permute-start = (bf16[16,96,128]{2,1,0:T(8,128)(2,1)S(1)}, bf16[16,96,128]{2,1,0:T(8,128)(2,1)S(1)}, u32[]{:S(2)}, u32[]{:S(2)}) collective-permute-start(bf16[16,96,128]{2,1,0:T(8,128)(2,1)S(1)} %all_to_all.10), channel_id=1, source_target_pairs={{0,1},{1,0},{2,3},{3,2},{4,5},{5,4},{6,7},{7,6},{8,9},{9,8},{10,11... | collective-permute-start | bytes 1179656 | tf_op jit(solution)/shard_map/ppermute | solution.py:214
  20.4 10.8 %collective-permute-start.1 = (bf16[1024,128]{1,0:T(8,128)(2,1)S(1)}, bf16[1024,128]{1,0:T(8,128)(2,1)S(1)}, u32[]{:S(2)}, u32[]{:S(2)}) collective-permute-start(bf16[1024,128]{1,0:T(8,128)(2,1)S(1)} %bitcast.2), channel_id=1, source_target_pairs={{0,2},{1,15},{2,0},{3,5},{4,6},{5,3},{6,4},{7,9},{8,10},{9,7},{10,... | collective-permute-start | bytes 786440 | tf_op jit(solution)/shard_map/ppermute | solution.py:203
  26.1 8.0 %collective-permute-start.3 = (bf16[1024,128]{1,0:T(8,128)(2,1)S(1)}, bf16[1024,128]{1,0:T(8,128)(2,1)S(1)}, u32[]{:S(2)}, u32[]{:S(2)}) collective-permute-start(bf16[1024,128]{1,0:T(8,128)(2,1)S(1)} %bitcast.5), channel_id=1, source_target_pairs={{0,2},{1,15},{2,0},{3,5},{4,6},{5,3},{6,4},{7,9},{8,10},{9,7},{10,... | collective-permute-start | bytes 786440 | tf_op jit(solution)/shard_map/ppermute | solution.py:203
  31.2 7.1 %collective-permute-start.2 = (bf16[1024,128]{1,0:T(8,128)(2,1)S(1)}, bf16[1024,128]{1,0:T(8,128)(2,1)S(1)}, u32[]{:S(2)}, u32[]{:S(2)}) collective-permute-start(bf16[1024,128]{1,0:T(8,128)(2,1)S(1)} %collective-permute-done.1.kv_ref.refs_1_), channel_id=1, source_target_pairs={{0,14},{1,3},{2,4},{3,1},{4,2},{5,7},{6,8},{7,5},{8,6},{9,11},{10,... | collective-permute-start | bytes 786440 | tf_op jit(solution)/shard_map/ppermute | solution.py:203
  34.0 8.6 %collective-permute-start.5 = (bf16[1024,128]{1,0:T(8,128)(2,1)S(1)}, bf16[1024,128]{1,0:T(8,128)(2,1)S(1)}, u32[]{:S(2)}, u32[]{:S(2)}) collective-permute-start(bf16[1024,128]{1,0:T(8,128)(2,1)S(1)} %collective-permute-done.3.kv_ref.refs_2_), channel_id=1, source_target_pairs={{0,14},{1,3},{2,4},{3,1},{4,2},{5,7},{6,8},{7,5},{8,6},{9,11},{10,... | collective-permute-start | bytes 786440 | tf_op jit(solution)/shard_map/ppermute | solution.py:203
  38.3 8.4 %collective-permute-start.4 = (bf16[1024,128]{1,0:T(8,128)(2,1)S(1)}, bf16[1024,128]{1,0:T(8,128)(2,1)S(1)}, u32[]{:S(2)}, u32[]{:S(2)}) collective-permute-start(bf16[1024,128]{1,0:T(8,128)(2,1)S(1)} %collective-permute-done.2.kv_ref.refs_3_), channel_id=1, source_target_pairs={{0,2},{1,15},{2,0},{3,5},{4,6},{5,3},{6,4},{7,9},{8,10},{9,7},{10,... | collective-permute-start | bytes 786440 | tf_op jit(solution)/shard_map/ppermute | solution.py:203
  42.7 7.1 %collective-permute-start.7 = (bf16[1024,128]{1,0:T(8,128)(2,1)S(1)}, bf16[1024,128]{1,0:T(8,128)(2,1)S(1)}, u32[]{:S(2)}, u32[]{:S(2)}) collective-permute-start(bf16[1024,128]{1,0:T(8,128)(2,1)S(1)} %collective-permute-done.5.kv_ref.refs_4_), channel_id=1, source_target_pairs={{0,2},{1,15},{2,0},{3,5},{4,6},{5,3},{6,4},{7,9},{8,10},{9,7},{10,... | collective-permute-start | bytes 786440 | tf_op jit(solution)/shard_map/ppermute | solution.py:203
  46.7 6.0 %collective-permute-start.6 = (bf16[1024,128]{1,0:T(8,128)(2,1)S(1)}, bf16[1024,128]{1,0:T(8,128)(2,1)S(1)}, u32[]{:S(2)}, u32[]{:S(2)}) collective-permute-start(bf16[1024,128]{1,0:T(8,128)(2,1)S(1)} %collective-permute-done.4.kv_ref.refs_5_), channel_id=1, source_target_pairs={{0,14},{1,3},{2,4},{3,1},{4,2},{5,7},{6,8},{7,5},{8,6},{9,11},{10,... | collective-permute-start | bytes 786440 | tf_op jit(solution)/shard_map/ppermute | solution.py:203
  107.3 14.8 %copy-start = (bf16[1024,1024]{1,0:T(8,128)(2,1)S(1)}, bf16[1024,1024]{1,0:T(8,128)(2,1)}, u32[]{:S(2)}) copy-start(bf16[1024,1024]{1,0:T(8,128)(2,1)} %w_ref.1) | copy-start | bytes 6291460
  107.3 4.2 %collective-permute-start.8 = (f32[1024,128]{1,0:T(8,128)S(1)}, f32[1024,128]{1,0:T(8,128)S(1)}, u32[]{:S(2)}, u32[]{:S(2)}) collective-permute-start(f32[1024,128]{1,0:T(8,128)S(1)} %get-tuple-element.33), channel_id=1, source_target_pairs={{0,1},{1,0},{2,3},{3,2},{4,5},{5,4},{6,7},{7,6},{8,9},{9,8},{10,11... | collective-permute-start | bytes 1572872 | tf_op jit(solution)/shard_map/ppermute | solution.py:239

commit v5 on v2

--- a/solution.py
+++ b/solution.py
@@ -191,11 +191,9 @@
         lambda z: (z + 1) % deep if z % 2 else (z - 1) % deep,
     )
 
-    def exchanged(block, hop):
-        pairs = [
-            (2 * z + c, 2 * pairings[(hop + c) % 2](z) + c) for z in range(deep) for c in range(2)
-        ]
-        return lax.ppermute(block, ("zh", "zl", "c"), pairs)
+    def exchanged(block, turn):
+        pairs = [(z, pairings[turn % 2](z)) for z in range(deep)]
+        return lax.ppermute(block, ("zh", "zl"), pairs)
 
     def cost(blocks):
         return pl.CostEstimate(
@@ -207,7 +205,7 @@
     q_shape, acc_shape = shape((2 * count, LANES), bf16), shape((2 * count, LANES), f32)
     chains = [exchanged(kv, 0)]
     partners = lax.ppermute(mine, "c", swap)
-    chains.append(exchanged(partners[:, :rows].reshape(count, LANES), 0))
+    chains.append(exchanged(partners[:, :rows].reshape(count, LANES), 1))
     q_all, acc = call(first_kernel, q_shape, acc_shape, cost_estimate=cost(1))(
         mine[:, rows:], partners[:, rows:], kv
     )
@@ -217,7 +215,7 @@
             now, acc = lax.optimization_barrier((chains[n], acc))
             blocks.append(now)
             if n == 0 or hop + 1 < deep // 2:
-                chains[n] = exchanged(now, hop)
+                chains[n] = exchanged(now, hop + n)
             acc = call(
                 step_kernel, acc_shape, cost_estimate=cost(1), input_output_aliases={2: 0}
             )(q_all, now, acc)

time: 123 us -> 128 us (1.041)
  waiting for transfers between devices: 1.73 us -> 6.49 us
    ppermute x7, waiting for transfers between devices: 0.19 us -> 4.95 us  [exchanged(): return lax.ppermute(block, ('zh', 'zl'), pairs)]
  transfers between devices with their start and end apart: 9 -> 9, of which waited for: 2 -> 4; matrix products, arithmetic and copies ran while one was open for 0% -> 0% of each run, Pallas kernels for 16% -> 16%
where the time goes in v5:
time: 128 us
  Pallas kernels  78.5 us (61%)
  blocking collectives  25.8 us (20%)
  starting transfers between devices  17.2 us (13%)
  waiting for transfers between devices  6.49 us (5%)
    pallas_call x1, Pallas kernels, on_device(): call(last_kernel, acc_shape, in_specs=[vmem] * 3 + [anywhere] * len(block...  54.5 us
    pallas_call x6, Pallas kernels, on_device(): call(step_kernel, acc_shape, cost_estimate=cost(1), input_output_aliases=...  16.4 us
    all_to_all x1, blocking collectives, on_device(): mine = lax.all_to_all(packed, ('x', 'y'), 0, 0, tiled=True)  15.9 us
    ppermute x7, starting transfers between devices, exchanged(): return lax.ppermute(block, ('zh', 'zl'), pairs)  12.9 us
    all_to_all x1, blocking collectives, on_device(): heads = lax.all_to_all(attended, ('x', 'y'), 0, 0, tiled=True)  9.93 us
    ppermute x7, waiting for transfers between devices, exchanged(): return lax.ppermute(block, ('zh', 'zl'), pairs)  4.95 us
    pallas_call x1, Pallas kernels, on_device(): call(first_kernel, q_shape, acc_shape, cost_estimate=cost(1))  3.77 us
  transfers between devices with their start and end apart: 9, of which 4 were waited for; matrix products, arithmetic and copies ran while one was open for 0% of the time, Pallas kernels for 16%

profile of v5, /device:TPU:1, one launch (start us, length us, event | category | flops | bytes accessed | tf_op | source)
XLA Modules:
  0.0 128.3 jit_solution(7597714390156229281)
XLA Ops:
  0.0 2.0 %shard_map.46 = bf16[16,96,128]{2,1,0:T(8,128)(2,1)} custom-call(bf16[64,1024]{1,0:T(8,128)(2,1)} %q_hbm.1, bf16[64,1024]{1,0:T(8,128)(2,1)} %k_hbm.1, bf16[64,1024]{1,0:T(8,128)(2,1)} %v_hbm.1), custom_call_target="tpu_custom_call" | custom-call | tf_op jit(solution)/shard_map/pallas_call | solution.py:175
  2.0 15.9 %all_to_all.10 = bf16[16,96,128]{2,1,0:T(8,128)(2,1)S(1)} all-to-all(bf16[16,96,128]{2,1,0:T(8,128)(2,1)} %shard_map.46), channel_id=1, replica_groups=mesh['x'=4,'y'=4,'zh'=2,'zl'=4,'c'=2] {'x','y'}, dimensions={0} | all-to-all | bytes 786432 | tf_op jit(solution)/shard_map/all_to_all | solution.py:183
  17.8 2.5 %collective-permute-start = (bf16[16,96,128]{2,1,0:T(8,128)(2,1)S(1)}, bf16[16,96,128]{2,1,0:T(8,128)(2,1)S(1)}, u32[]{:S(2)}, u32[]{:S(2)}) collective-permute-start(bf16[16,96,128]{2,1,0:T(8,128)(2,1)S(1)} %all_to_all.10), channel_id=1, source_target_pairs={{0,1},{1,0},{2,3},{3,2},{4,5},{5,4},{6,7},{7,6},{8,9},{9,8},{10,11... | collective-permute-start | bytes 1179656 | tf_op jit(solution)/shard_map/ppermute | solution.py:207
  20.4 1.7 %collective-permute-start.1 = (bf16[1024,128]{1,0:T(8,128)(2,1)S(1)}, bf16[1024,128]{1,0:T(8,128)(2,1)S(1)}, u32[]{:S(2)}, u32[]{:S(2)}) collective-permute-start(bf16[1024,128]{1,0:T(8,128)(2,1)S(1)} %bitcast.2), channel_id=1, source_target_pairs={{0,2},{2,0},{4,6},{6,4},{8,10},{10,8},{12,14},{14,12},{1,3},{3,1},... | collective-permute-start | bytes 786440 | tf_op jit(solution)/shard_map/ppermute | solution.py:196
  22.1 0.0 collective-permute-done
  22.1 5.2 %collective-permute-start.3 = (bf16[1024,128]{1,0:T(8,128)(2,1)S(1)}, bf16[1024,128]{1,0:T(8,128)(2,1)S(1)}, u32[]{:S(2)}, u32[]{:S(2)}) collective-permute-start(bf16[1024,128]{1,0:T(8,128)(2,1)S(1)} %bitcast.5), channel_id=1, source_target_pairs={{0,14},{2,4},{4,2},{6,8},{8,6},{10,12},{12,10},{14,0},{1,15},{3,5}... | collective-permute-start | bytes 786440 | tf_op jit(solution)/shard_map/ppermute | solution.py:196
  27.4 3.8 %shard_map.47 = (bf16[2048,128]{1,0:T(8,128)(2,1)S(1)}, f32[2048,128]{1,0:T(8,128)S(1)}) custom-call(bf16[16,32,128]{2,1,0:T(8,128)(2,1)S(1)} %slice.24.q_own_ref, bf16[16,32,128]{2,1,0:T(8,128)(2,1)S(1)} %slice.25.q_other_ref, bf16[1024,128]{1,0:T(8,128)(2,1)S(1)} %bitcast.3), custom_call_target="tpu_custom_call" | custom-call | flops 2147483648 | bytes 4194304 | tf_op jit(solution)/shard_map/pallas_call | solution.py:209
  31.2 0.0 collective-permute-done.1.kv_ref.refs_1_
  31.2 2.8 %collective-permute-start.2 = (bf16[1024,128]{1,0:T(8,128)(2,1)S(1)}, bf16[1024,128]{1,0:T(8,128)(2,1)S(1)}, u32[]{:S(2)}, u32[]{:S(2)}) collective-permute-start(bf16[1024,128]{1,0:T(8,128)(2,1)S(1)} %collective-permute-done.1.kv_ref.refs_1_), channel_id=1, source_target_pairs={{0,14},{2,4},{4,2},{6,8},{8,6},{10,12},{12,10},{14,0},{1,15},{3,5}... | collective-permute-start | bytes 786440 | tf_op jit(solution)/shard_map/ppermute | solution.py:196
  34.0 2.7 %shard_map.48.acc_in_ref = f32[2048,128]{1,0:T(8,128)S(1)} custom-call(bf16[2048,128]{1,0:T(8,128)(2,1)S(1)} %get-tuple-element.19.q_ref, bf16[1024,128]{1,0:T(8,128)(2,1)S(1)} %collective-permute-done.1.kv_ref.refs_1_, f32[2048,128]{1,0:T(8,128)S(1)} %get-tuple-element.22.acc_in_ref), custom_call_target="tpu_custom_call", output_to_operand_aliasing={{}: (2, {})} | custom-call | flops 2147483648 | bytes 4194304 | tf_op jit(solution)/shard_map/pallas_call | solution.py:219
  36.7 0.0 collective-permute-done.3.kv_ref.refs_2_
  36.7 0.1 collective-permute-start.5
  36.8 2.7 %shard_map.49.acc_in_ref = f32[2048,128]{1,0:T(8,128)S(1)} custom-call(bf16[2048,128]{1,0:T(8,128)(2,1)S(1)} %get-tuple-element.19.q_ref, bf16[1024,128]{1,0:T(8,128)(2,1)S(1)} %collective-permute-done.3.kv_ref.refs_2_, f32[2048,128]{1,0:T(8,128)S(1)} %shard_map.48.acc_in_ref), custom_call_target="tpu_custom_call", output_to_operand_aliasing={{}: (2, {})} | custom-call | flops 2147483648 | bytes 4194304 | tf_op jit(solution)/shard_map/pallas_call | solution.py:219
  39.6 0.2 collective-permute-done.2.kv_ref.refs_3_
  39.7 1.4 %collective-permute-start.4 = (bf16[1024,128]{1,0:T(8,128)(2,1)S(1)}, bf16[1024,128]{1,0:T(8,128)(2,1)S(1)}, u32[]{:S(2)}, u32[]{:S(2)}) collective-permute-start(bf16[1024,128]{1,0:T(8,128)(2,1)S(1)} %collective-permute-done.2.kv_ref.refs_3_), channel_id=1, source_target_pairs={{0,2},{2,0},{4,6},{6,4},{8,10},{10,8},{12,14},{14,12},{1,3},{3,1},... | collective-permute-start | bytes 786440 | tf_op jit(solution)/shard_map/ppermute | solution.py:196
  41.1 2.7 %shard_map.50.acc_in_ref = f32[2048,128]{1,0:T(8,128)S(1)} custom-call(bf16[2048,128]{1,0:T(8,128)(2,1)S(1)} %get-tuple-element.19.q_ref, bf16[1024,128]{1,0:T(8,128)(2,1)S(1)} %collective-permute-done.2.kv_ref.refs_3_, f32[2048,128]{1,0:T(8,128)S(1)} %shard_map.49.acc_in_ref), custom_call_target="tpu_custom_call", output_to_operand_aliasing={{}: (2, {})} | custom-call | flops 2147483648 | bytes 4194304 | tf_op jit(solution)/shard_map/pallas_call | solution.py:219
  43.9 0.0 collective-permute-done.5.kv_ref.refs_4_
  43.9 1.2 collective-permute-start.7
  45.1 2.7 %shard_map.51.acc_in_ref = f32[2048,128]{1,0:T(8,128)S(1)} custom-call(bf16[2048,128]{1,0:T(8,128)(2,1)S(1)} %get-tuple-element.19.q_ref, bf16[1024,128]{1,0:T(8,128)(2,1)S(1)} %collective-permute-done.5.kv_ref.refs_4_, f32[2048,128]{1,0:T(8,128)S(1)} %shard_map.50.acc_in_ref), custom_call_target="tpu_custom_call", output_to_operand_aliasing={{}: (2, {})} | custom-call | flops 2147483648 | bytes 4194304 | tf_op jit(solution)/shard_map/pallas_call | solution.py:219
  47.8 1.3 %collective-permute-done.4.kv_ref.refs_5_ = bf16[1024,128]{1,0:T(8,128)(2,1)S(1)} collective-permute-done((bf16[1024,128]{1,0:T(8,128)(2,1)S(1)}, bf16[1024,128]{1,0:T(8,128)(2,1)S(1)}, u32[]{:S(2)}, u32[]{:S(2)}) %collective-permute-start.4) | collective-permute-done | bytes 262176 | tf_op jit(solution)/shard_map/ppermute | solution.py:196
  49.2 0.5 collective-permute-start.6
  49.7 2.7 %shard_map.52.acc_in_ref = f32[2048,128]{1,0:T(8,128)S(1)} custom-call(bf16[2048,128]{1,0:T(8,128)(2,1)S(1)} %get-tuple-element.19.q_ref, bf16[1024,128]{1,0:T(8,128)(2,1)S(1)} %collective-permute-done.4.kv_ref.refs_5_, f32[2048,128]{1,0:T(8,128)S(1)} %shard_map.51.acc_in_ref), custom_call_target="tpu_custom_call", output_to_operand_aliasing={{}: (2, {})} | custom-call | flops 2147483648 | bytes 4194304 | tf_op jit(solution)/shard_map/pallas_call | solution.py:219
  52.4 0.0 collective-permute-done.7.kv_ref.refs_6_
  52.4 2.7 %shard_map.53.acc_in_ref = f32[2048,128]{1,0:T(8,128)S(1)} custom-call(bf16[2048,128]{1,0:T(8,128)(2,1)S(1)} %get-tuple-element.19.q_ref, bf16[1024,128]{1,0:T(8,128)(2,1)S(1)} %collective-permute-done.7.kv_ref.refs_6_, f32[2048,128]{1,0:T(8,128)S(1)} %shard_map.52.acc_in_ref), custom_call_target="tpu_custom_call", output_to_operand_aliasing={{}: (2, {})} | custom-call | flops 2147483648 | bytes 4194304 | tf_op jit(solution)/shard_map/pallas_call | solution.py:219
  55.2 3.4 %collective-permute-done.6.kv_ref.refs_7_ = bf16[1024,128]{1,0:T(8,128)(2,1)S(1)} collective-permute-done((bf16[1024,128]{1,0:T(8,128)(2,1)S(1)}, bf16[1024,128]{1,0:T(8,128)(2,1)S(1)}, u32[]{:S(2)}, u32[]{:S(2)}) %collective-permute-start.6) | collective-permute-done | bytes 262176 | tf_op jit(solution)/shard_map/ppermute | solution.py:196
  58.6 54.5 %shard_map.54 = f32[2048,128]{1,0:T(8,128)S(1)} custom-call(bf16[2048,128]{1,0:T(8,128)(2,1)S(1)} %get-tuple-element.19.q_ref, bf16[1024,128]{1,0:T(8,128)(2,1)S(1)} %collective-permute-done.6.kv_ref.refs_7_, f32[2048,128]{1,0:T(8,128)S(1)} %shard_map.53.acc_in_ref, bf16[1024,128]{1,0:T(8,128)(2,1)S(1)} %bitcast.4, ...), custom_call_target="tpu_custom_call", output_to_operand_aliasing={{}: (2, {})} | custom-call | flops 2147483648 | bytes 4194304 | tf_op jit(solution)/shard_map/pallas_call | solution.py:223
  113.2 0.0 copy-start
  113.2 0.1 fusion
  113.3 1.8 %collective-permute-start.8 = (f32[1024,128]{1,0:T(8,128)S(1)}, f32[1024,128]{1,0:T(8,128)S(1)}, u32[]{:S(2)}, u32[]{:S(2)}) collective-permute-start(f32[1024,128]{1,0:T(8,128)S(1)} %get-tuple-element.33), channel_id=1, source_target_pairs={{0,1},{1,0},{2,3},{3,2},{4,5},{5,4},{6,7},{7,6},{8,9},{9,8},{10,11... | collective-permute-start | bytes 1572872 | tf_op jit(solution)/shard_map/ppermute | solution.py:232
  115.1 1.5 %collective-permute-done.8.other_ref = f32[1024,128]{1,0:T(8,128)S(1)} collective-permute-done((f32[1024,128]{1,0:T(8,128)S(1)}, f32[1024,128]{1,0:T(8,128)S(1)}, u32[]{:S(2)}, u32[]{:S(2)}) %collective-permute-start.8) | collective-permute-done | bytes 524320 | tf_op jit(solution)/shard_map/ppermute | solution.py:232
  116.6 0.6 shard_map.55
  117.1 9.9 %all_to_all.11.heads_ref = bf16[16,32,128]{2,1,0:T(8,128)(2,1)S(1)} all-to-all(bf16[16,32,128]{2,1,0:T(8,128)(2,1)S(1)} %shard_map.55), channel_id=1, replica_groups=mesh['x'=4,'y'=4,'zh'=2,'zl'=4,'c'=2] {'x','y'}, dimensions={0} | all-to-all | bytes 262144 | tf_op jit(solution)/shard_map/all_to_all | solution.py:235
  127.1 0.0 copy-done
  127.1 1.2 shard_map.56
  (4 shorter events, 0.1 us)
Async XLA Ops:
  17.8 4.3 %collective-permute-start = (bf16[16,96,128]{2,1,0:T(8,128)(2,1)S(1)}, bf16[16,96,128]{2,1,0:T(8,128)(2,1)S(1)}, u32[]{:S(2)}, u32[]{:S(2)}) collective-permute-start(bf16[16,96,128]{2,1,0:T(8,128)(2,1)S(1)} %all_to_all.10), channel_id=1, source_target_pairs={{0,1},{1,0},{2,3},{3,2},{4,5},{5,4},{6,7},{7,6},{8,9},{9,8},{10,11... | collective-permute-start | bytes 1179656 | tf_op jit(solution)/shard_map/ppermute | solution.py:207
  20.4 10.8 %collective-permute-start.1 = (bf16[1024,128]{1,0:T(8,128)(2,1)S(1)}, bf16[1024,128]{1,0:T(8,128)(2,1)S(1)}, u32[]{:S(2)}, u32[]{:S(2)}) collective-permute-start(bf16[1024,128]{1,0:T(8,128)(2,1)S(1)} %bitcast.2), channel_id=1, source_target_pairs={{0,2},{2,0},{4,6},{6,4},{8,10},{10,8},{12,14},{14,12},{1,3},{3,1},... | collective-permute-start | bytes 786440 | tf_op jit(solution)/shard_map/ppermute | solution.py:196
  22.1 14.6 %collective-permute-start.3 = (bf16[1024,128]{1,0:T(8,128)(2,1)S(1)}, bf16[1024,128]{1,0:T(8,128)(2,1)S(1)}, u32[]{:S(2)}, u32[]{:S(2)}) collective-permute-start(bf16[1024,128]{1,0:T(8,128)(2,1)S(1)} %bitcast.5), channel_id=1, source_target_pairs={{0,14},{2,4},{4,2},{6,8},{8,6},{10,12},{12,10},{14,0},{1,15},{3,5}... | collective-permute-start | bytes 786440 | tf_op jit(solution)/shard_map/ppermute | solution.py:196
  31.2 8.6 %collective-permute-start.2 = (bf16[1024,128]{1,0:T(8,128)(2,1)S(1)}, bf16[1024,128]{1,0:T(8,128)(2,1)S(1)}, u32[]{:S(2)}, u32[]{:S(2)}) collective-permute-start(bf16[1024,128]{1,0:T(8,128)(2,1)S(1)} %collective-permute-done.1.kv_ref.refs_1_), channel_id=1, source_target_pairs={{0,14},{2,4},{4,2},{6,8},{8,6},{10,12},{12,10},{14,0},{1,15},{3,5}... | collective-permute-start | bytes 786440 | tf_op jit(solution)/shard_map/ppermute | solution.py:196
  36.7 7.2 %collective-permute-start.5 = (bf16[1024,128]{1,0:T(8,128)(2,1)S(1)}, bf16[1024,128]{1,0:T(8,128)(2,1)S(1)}, u32[]{:S(2)}, u32[]{:S(2)}) collective-permute-start(bf16[1024,128]{1,0:T(8,128)(2,1)S(1)} %collective-permute-done.3.kv_ref.refs_2_), channel_id=1, source_target_pairs={{0,2},{2,0},{4,6},{6,4},{8,10},{10,8},{12,14},{14,12},{1,3},{3,1},... | collective-permute-start | bytes 786440 | tf_op jit(solution)/shard_map/ppermute | solution.py:196
  39.7 9.4 %collective-permute-start.4 = (bf16[1024,128]{1,0:T(8,128)(2,1)S(1)}, bf16[1024,128]{1,0:T(8,128)(2,1)S(1)}, u32[]{:S(2)}, u32[]{:S(2)}) collective-permute-start(bf16[1024,128]{1,0:T(8,128)(2,1)S(1)} %collective-permute-done.2.kv_ref.refs_3_), channel_id=1, source_target_pairs={{0,2},{2,0},{4,6},{6,4},{8,10},{10,8},{12,14},{14,12},{1,3},{3,1},... | collective-permute-start | bytes 786440 | tf_op jit(solution)/shard_map/ppermute | solution.py:196
  43.9 8.5 %collective-permute-start.7 = (bf16[1024,128]{1,0:T(8,128)(2,1)S(1)}, bf16[1024,128]{1,0:T(8,128)(2,1)S(1)}, u32[]{:S(2)}, u32[]{:S(2)}) collective-permute-start(bf16[1024,128]{1,0:T(8,128)(2,1)S(1)} %collective-permute-done.5.kv_ref.refs_4_), channel_id=1, source_target_pairs={{0,14},{2,4},{4,2},{6,8},{8,6},{10,12},{12,10},{14,0},{1,15},{3,5}... | collective-permute-start | bytes 786440 | tf_op jit(solution)/shard_map/ppermute | solution.py:196
  49.2 9.5 %collective-permute-start.6 = (bf16[1024,128]{1,0:T(8,128)(2,1)S(1)}, bf16[1024,128]{1,0:T(8,128)(2,1)S(1)}, u32[]{:S(2)}, u32[]{:S(2)}) collective-permute-start(bf16[1024,128]{1,0:T(8,128)(2,1)S(1)} %collective-permute-done.4.kv_ref.refs_5_), channel_id=1, source_target_pairs={{0,14},{2,4},{4,2},{6,8},{8,6},{10,12},{12,10},{14,0},{1,15},{3,5}... | collective-permute-start | bytes 786440 | tf_op jit(solution)/shard_map/ppermute | solution.py:196
  113.2 13.9 %copy-start = (bf16[1024,1024]{1,0:T(8,128)(2,1)S(1)}, bf16[1024,1024]{1,0:T(8,128)(2,1)}, u32[]{:S(2)}) copy-start(bf16[1024,1024]{1,0:T(8,128)(2,1)} %w_ref.1) | copy-start | bytes 6291460
  113.3 3.3 %collective-permute-start.8 = (f32[1024,128]{1,0:T(8,128)S(1)}, f32[1024,128]{1,0:T(8,128)S(1)}, u32[]{:S(2)}, u32[]{:S(2)}) collective-permute-start(f32[1024,128]{1,0:T(8,128)S(1)} %get-tuple-element.33), channel_id=1, source_target_pairs={{0,1},{1,0},{2,3},{3,2},{4,5},{5,4},{6,7},{7,6},{8,9},{9,8},{10,11... | collective-permute-start | bytes 1572872 | tf_op jit(solution)/shard_map/ppermute | solution.py:232

commit v6 on v4

--- a/solution.py
+++ b/solution.py
@@ -211,10 +211,11 @@
 
     q_shape, acc_shape = shape((2 * count, LANES), bf16), shape((2 * count, LANES), f32)
     chains = [exchanged(kv, 0)]
-    partners = lax.ppermute(mine, "c", swap)
-    chains.append(exchanged(partners[:, :rows].reshape(count, LANES), 0))
+    partner_kv = lax.ppermute(kv, "c", swap)
+    partner_q = lax.ppermute(mine[:, rows:], "c", swap)
+    chains.append(exchanged(partner_kv, 0))
     q_all, acc = call(first_kernel, q_shape, acc_shape, cost_estimate=cost(1))(
-        mine[:, rows:], partners[:, rows:], kv
+        mine[:, rows:], partner_q, kv
     )
     blocks = [kv]
     for hop in range(1, deep // 2):

time: 123 us -> 124 us (level)
    ppermute x1 -> x2, starting transfers between devices: 2.51 us -> 2.7 us  [the longest x1 2.6 us: on_device(): partner_kv = lax.ppermute(kv, 'c', swap)]
  transfers between devices with their start and end apart: 9 -> 10, of which waited for: 2 -> 2; matrix products, arithmetic and copies ran while one was open for 0% -> 0% of each run, Pallas kernels for 16% -> 16%
where the time goes in v6:
time: 124 us
  Pallas kernels  78.5 us (63%)
  blocking collectives  25.8 us (21%)
  starting transfers between devices  16.2 us (13%)
  waiting for transfers between devices  2.87 us (2%)
    pallas_call x1, Pallas kernels, on_device(): call(last_kernel, acc_shape, in_specs=[vmem] * 3 + [anywhere] * len(block...  54.6 us
    pallas_call x6, Pallas kernels, on_device(): call(step_kernel, acc_shape, cost_estimate=cost(1), input_output_aliases=...  16.4 us
    all_to_all x1, blocking collectives, on_device(): mine = lax.all_to_all(packed, ('x', 'y'), 0, 0, tiled=True)  15.9 us
    ppermute x7, starting transfers between devices, exchanged(): return lax.ppermute(block, ('zh', 'zl', 'c'), pairs)  11.4 us
    all_to_all x1, blocking collectives, on_device(): heads = lax.all_to_all(attended, ('x', 'y'), 0, 0, tiled=True)  9.93 us
    pallas_call x1, Pallas kernels, on_device(): call(first_kernel, q_shape, acc_shape, cost_estimate=cost(1))  3.77 us
    ppermute x1, starting transfers between devices, on_device(): partner_kv = lax.ppermute(kv, 'c', swap)  2.6 us
  transfers between devices with their start and end apart: 10, of which 2 were waited for; matrix products, arithmetic and copies ran while one was open for 0% of the time, Pallas kernels for 16%

profile of v6, /device:TPU:1, one launch (start us, length us, event | category | flops | bytes accessed | tf_op | source)
XLA Modules:
  0.0 123.6 jit_solution(14926573872595230741)
XLA Ops:
  0.0 2.0 %shard_map.46 = bf16[16,96,128]{2,1,0:T(8,128)(2,1)} custom-call(bf16[64,1024]{1,0:T(8,128)(2,1)} %q_hbm.1, bf16[64,1024]{1,0:T(8,128)(2,1)} %k_hbm.1, bf16[64,1024]{1,0:T(8,128)(2,1)} %v_hbm.1), custom_call_target="tpu_custom_call" | custom-call | tf_op jit(solution)/shard_map/pallas_call | solution.py:180
  2.0 15.9 %all_to_all.10 = bf16[16,96,128]{2,1,0:T(8,128)(2,1)S(1)} all-to-all(bf16[16,96,128]{2,1,0:T(8,128)(2,1)} %shard_map.46), channel_id=1, replica_groups=mesh['x'=4,'y'=4,'zh'=2,'zl'=4,'c'=2] {'x','y'}, dimensions={0} | all-to-all | bytes 786432 | tf_op jit(solution)/shard_map/all_to_all | solution.py:188
  17.9 2.6 %collective-permute-start.3 = (bf16[1024,128]{1,0:T(8,128)(2,1)S(1)}, bf16[1024,128]{1,0:T(8,128)(2,1)S(1)}, u32[]{:S(2)}, u32[]{:S(2)}) collective-permute-start(bf16[1024,128]{1,0:T(8,128)(2,1)S(1)} %bitcast.1), channel_id=1, source_target_pairs={{0,1},{1,0},{2,3},{3,2},{4,5},{5,4},{6,7},{7,6},{8,9},{9,8},{10,11... | collective-permute-start | bytes 786440 | tf_op jit(solution)/shard_map/ppermute | solution.py:214
  20.5 0.1 collective-permute-start
  20.6 5.7 %collective-permute-start.1 = (bf16[1024,128]{1,0:T(8,128)(2,1)S(1)}, bf16[1024,128]{1,0:T(8,128)(2,1)S(1)}, u32[]{:S(2)}, u32[]{:S(2)}) collective-permute-start(bf16[1024,128]{1,0:T(8,128)(2,1)S(1)} %bitcast.2), channel_id=1, source_target_pairs={{0,2},{1,15},{2,0},{3,5},{4,6},{5,3},{6,4},{7,9},{8,10},{9,7},{10,... | collective-permute-start | bytes 786440 | tf_op jit(solution)/shard_map/ppermute | solution.py:203
  26.2 0.0 collective-permute-done.3
  26.2 1.0 collective-permute-start.4
  27.2 0.0 collective-permute-done.q_other_ref
  27.2 3.8 %shard_map.47 = (bf16[2048,128]{1,0:T(8,128)(2,1)S(1)}, f32[2048,128]{1,0:T(8,128)S(1)}) custom-call(bf16[16,32,128]{2,1,0:T(8,128)(2,1)S(1)} %slice.17.q_own_ref, bf16[16,32,128]{2,1,0:T(8,128)(2,1)S(1)} %collective-permute-done.q_other_ref, bf16[1024,128]{1,0:T(8,128)(2,1)S(1)} %bitcast.3), custom_call_target="tpu_custom_call" | custom-call | flops 2147483648 | bytes 4194304 | tf_op jit(solution)/shard_map/pallas_call | solution.py:217
  31.0 0.0 collective-permute-done.1.kv_ref.refs_1_
  31.0 0.1 collective-permute-start.2
  31.1 2.7 %shard_map.48.acc_in_ref = f32[2048,128]{1,0:T(8,128)S(1)} custom-call(bf16[2048,128]{1,0:T(8,128)(2,1)S(1)} %get-tuple-element.19.q_ref, bf16[1024,128]{1,0:T(8,128)(2,1)S(1)} %collective-permute-done.1.kv_ref.refs_1_, f32[2048,128]{1,0:T(8,128)S(1)} %get-tuple-element.22.acc_in_ref), custom_call_target="tpu_custom_call", output_to_operand_aliasing={{}: (2, {})} | custom-call | flops 2147483648 | bytes 4194304 | tf_op jit(solution)/shard_map/pallas_call | solution.py:227
  33.8 0.0 collective-permute-done.4.kv_ref.refs_2_
  33.8 1.5 %collective-permute-start.6 = (bf16[1024,128]{1,0:T(8,128)(2,1)S(1)}, bf16[1024,128]{1,0:T(8,128)(2,1)S(1)}, u32[]{:S(2)}, u32[]{:S(2)}) collective-permute-start(bf16[1024,128]{1,0:T(8,128)(2,1)S(1)} %collective-permute-done.4.kv_ref.refs_2_), channel_id=1, source_target_pairs={{0,14},{1,3},{2,4},{3,1},{4,2},{5,7},{6,8},{7,5},{8,6},{9,11},{10,... | collective-permute-start | bytes 786440 | tf_op jit(solution)/shard_map/ppermute | solution.py:203
  35.4 2.7 %shard_map.49.acc_in_ref = f32[2048,128]{1,0:T(8,128)S(1)} custom-call(bf16[2048,128]{1,0:T(8,128)(2,1)S(1)} %get-tuple-element.19.q_ref, bf16[1024,128]{1,0:T(8,128)(2,1)S(1)} %collective-permute-done.4.kv_ref.refs_2_, f32[2048,128]{1,0:T(8,128)S(1)} %shard_map.48.acc_in_ref), custom_call_target="tpu_custom_call", output_to_operand_aliasing={{}: (2, {})} | custom-call | flops 2147483648 | bytes 4194304 | tf_op jit(solution)/shard_map/pallas_call | solution.py:227
  38.1 0.0 collective-permute-done.2.kv_ref.refs_3_
  38.1 1.8 %collective-permute-start.5 = (bf16[1024,128]{1,0:T(8,128)(2,1)S(1)}, bf16[1024,128]{1,0:T(8,128)(2,1)S(1)}, u32[]{:S(2)}, u32[]{:S(2)}) collective-permute-start(bf16[1024,128]{1,0:T(8,128)(2,1)S(1)} %collective-permute-done.2.kv_ref.refs_3_), channel_id=1, source_target_pairs={{0,2},{1,15},{2,0},{3,5},{4,6},{5,3},{6,4},{7,9},{8,10},{9,7},{10,... | collective-permute-start | bytes 786440 | tf_op jit(solution)/shard_map/ppermute | solution.py:203
  39.9 2.7 %shard_map.50.acc_in_ref = f32[2048,128]{1,0:T(8,128)S(1)} custom-call(bf16[2048,128]{1,0:T(8,128)(2,1)S(1)} %get-tuple-element.19.q_ref, bf16[1024,128]{1,0:T(8,128)(2,1)S(1)} %collective-permute-done.2.kv_ref.refs_3_, f32[2048,128]{1,0:T(8,128)S(1)} %shard_map.49.acc_in_ref), custom_call_target="tpu_custom_call", output_to_operand_aliasing={{}: (2, {})} | custom-call | flops 2147483648 | bytes 4194304 | tf_op jit(solution)/shard_map/pallas_call | solution.py:227
  42.7 0.0 collective-permute-done.6.kv_ref.refs_4_
  42.7 1.2 collective-permute-start.8
  43.9 2.7 %shard_map.51.acc_in_ref = f32[2048,128]{1,0:T(8,128)S(1)} custom-call(bf16[2048,128]{1,0:T(8,128)(2,1)S(1)} %get-tuple-element.19.q_ref, bf16[1024,128]{1,0:T(8,128)(2,1)S(1)} %collective-permute-done.6.kv_ref.refs_4_, f32[2048,128]{1,0:T(8,128)S(1)} %shard_map.50.acc_in_ref), custom_call_target="tpu_custom_call", output_to_operand_aliasing={{}: (2, {})} | custom-call | flops 2147483648 | bytes 4194304 | tf_op jit(solution)/shard_map/pallas_call | solution.py:227
  46.7 0.0 collective-permute-done.5.kv_ref.refs_5_
  46.7 0.1 collective-permute-start.7
  46.8 2.7 %shard_map.52.acc_in_ref = f32[2048,128]{1,0:T(8,128)S(1)} custom-call(bf16[2048,128]{1,0:T(8,128)(2,1)S(1)} %get-tuple-element.19.q_ref, bf16[1024,128]{1,0:T(8,128)(2,1)S(1)} %collective-permute-done.5.kv_ref.refs_5_, f32[2048,128]{1,0:T(8,128)S(1)} %shard_map.51.acc_in_ref), custom_call_target="tpu_custom_call", output_to_operand_aliasing={{}: (2, {})} | custom-call | flops 2147483648 | bytes 4194304 | tf_op jit(solution)/shard_map/pallas_call | solution.py:227
  49.5 0.0 collective-permute-done.8.kv_ref.refs_6_
  49.6 2.7 %shard_map.53.acc_in_ref = f32[2048,128]{1,0:T(8,128)S(1)} custom-call(bf16[2048,128]{1,0:T(8,128)(2,1)S(1)} %get-tuple-element.19.q_ref, bf16[1024,128]{1,0:T(8,128)(2,1)S(1)} %collective-permute-done.8.kv_ref.refs_6_, f32[2048,128]{1,0:T(8,128)S(1)} %shard_map.52.acc_in_ref), custom_call_target="tpu_custom_call", output_to_operand_aliasing={{}: (2, {})} | custom-call | flops 2147483648 | bytes 4194304 | tf_op jit(solution)/shard_map/pallas_call | solution.py:227
  52.3 1.3 %collective-permute-done.7.kv_ref.refs_7_ = bf16[1024,128]{1,0:T(8,128)(2,1)S(1)} collective-permute-done((bf16[1024,128]{1,0:T(8,128)(2,1)S(1)}, bf16[1024,128]{1,0:T(8,128)(2,1)S(1)}, u32[]{:S(2)}, u32[]{:S(2)}) %collective-permute-start.7) | collective-permute-done | bytes 262176 | tf_op jit(solution)/shard_map/ppermute | solution.py:203
  53.6 54.6 %shard_map.54 = f32[2048,128]{1,0:T(8,128)S(1)} custom-call(bf16[2048,128]{1,0:T(8,128)(2,1)S(1)} %get-tuple-element.19.q_ref, bf16[1024,128]{1,0:T(8,128)(2,1)S(1)} %collective-permute-done.7.kv_ref.refs_7_, f32[2048,128]{1,0:T(8,128)S(1)} %shard_map.53.acc_in_ref, bf16[1024,128]{1,0:T(8,128)(2,1)S(1)} %bitcast.4, ...), custom_call_target="tpu_custom_call", output_to_operand_aliasing={{}: (2, {})} | custom-call | flops 2147483648 | bytes 4194304 | tf_op jit(solution)/shard_map/pallas_call | solution.py:231
  108.2 0.0 copy-start
  108.2 0.1 fusion
  108.3 2.1 %collective-permute-start.9 = (f32[1024,128]{1,0:T(8,128)S(1)}, f32[1024,128]{1,0:T(8,128)S(1)}, u32[]{:S(2)}, u32[]{:S(2)}) collective-permute-start(f32[1024,128]{1,0:T(8,128)S(1)} %get-tuple-element.33), channel_id=1, source_target_pairs={{0,1},{1,0},{2,3},{3,2},{4,5},{5,4},{6,7},{7,6},{8,9},{9,8},{10,11... | collective-permute-start | bytes 1572872 | tf_op jit(solution)/shard_map/ppermute | solution.py:240
  110.4 1.5 %collective-permute-done.9.other_ref = f32[1024,128]{1,0:T(8,128)S(1)} collective-permute-done((f32[1024,128]{1,0:T(8,128)S(1)}, f32[1024,128]{1,0:T(8,128)S(1)}, u32[]{:S(2)}, u32[]{:S(2)}) %collective-permute-start.9) | collective-permute-done | bytes 524320 | tf_op jit(solution)/shard_map/ppermute | solution.py:240
  111.9 0.6 shard_map.55
  112.5 9.9 %all_to_all.11.heads_ref = bf16[16,32,128]{2,1,0:T(8,128)(2,1)S(1)} all-to-all(bf16[16,32,128]{2,1,0:T(8,128)(2,1)S(1)} %shard_map.55), channel_id=1, replica_groups=mesh['x'=4,'y'=4,'zh'=2,'zl'=4,'c'=2] {'x','y'}, dimensions={0} | all-to-all | bytes 262144 | tf_op jit(solution)/shard_map/all_to_all | solution.py:243
  122.4 0.0 copy-done
  122.4 1.2 shard_map.56
  (2 shorter events, 0.0 us)
Async XLA Ops:
  17.9 8.4 %collective-permute-start.3 = (bf16[1024,128]{1,0:T(8,128)(2,1)S(1)}, bf16[1024,128]{1,0:T(8,128)(2,1)S(1)}, u32[]{:S(2)}, u32[]{:S(2)}) collective-permute-start(bf16[1024,128]{1,0:T(8,128)(2,1)S(1)} %bitcast.1), channel_id=1, source_target_pairs={{0,1},{1,0},{2,3},{3,2},{4,5},{5,4},{6,7},{7,6},{8,9},{9,8},{10,11... | collective-permute-start | bytes 786440 | tf_op jit(solution)/shard_map/ppermute | solution.py:214
  20.5 6.7 %collective-permute-start = (bf16[16,32,128]{2,1,0:T(8,128)(2,1)S(1)}, bf16[16,32,128]{2,1,0:T(8,128)(2,1)S(1)}, u32[]{:S(2)}, u32[]{:S(2)}) collective-permute-start(bf16[16,32,128]{2,1,0:T(8,128)(2,1)S(1)} %slice.17.q_own_ref), channel_id=1, source_target_pairs={{0,1},{1,0},{2,3},{3,2},{4,5},{5,4},{6,7},{7,6},{8,9},{9,8},{10,11... | collective-permute-start | bytes 393224 | tf_op jit(solution)/shard_map/ppermute | solution.py:215
  20.6 10.4 %collective-permute-start.1 = (bf16[1024,128]{1,0:T(8,128)(2,1)S(1)}, bf16[1024,128]{1,0:T(8,128)(2,1)S(1)}, u32[]{:S(2)}, u32[]{:S(2)}) collective-permute-start(bf16[1024,128]{1,0:T(8,128)(2,1)S(1)} %bitcast.2), channel_id=1, source_target_pairs={{0,2},{1,15},{2,0},{3,5},{4,6},{5,3},{6,4},{7,9},{8,10},{9,7},{10,... | collective-permute-start | bytes 786440 | tf_op jit(solution)/shard_map/ppermute | solution.py:203
  26.2 7.6 %collective-permute-start.4 = (bf16[1024,128]{1,0:T(8,128)(2,1)S(1)}, bf16[1024,128]{1,0:T(8,128)(2,1)S(1)}, u32[]{:S(2)}, u32[]{:S(2)}) collective-permute-start(bf16[1024,128]{1,0:T(8,128)(2,1)S(1)} %collective-permute-done.3), channel_id=1, source_target_pairs={{0,2},{1,15},{2,0},{3,5},{4,6},{5,3},{6,4},{7,9},{8,10},{9,7},{10,... | collective-permute-start | bytes 786440 | tf_op jit(solution)/shard_map/ppermute | solution.py:203
  31.0 7.1 %collective-permute-start.2 = (bf16[1024,128]{1,0:T(8,128)(2,1)S(1)}, bf16[1024,128]{1,0:T(8,128)(2,1)S(1)}, u32[]{:S(2)}, u32[]{:S(2)}) collective-permute-start(bf16[1024,128]{1,0:T(8,128)(2,1)S(1)} %collective-permute-done.1.kv_ref.refs_1_), channel_id=1, source_target_pairs={{0,14},{1,3},{2,4},{3,1},{4,2},{5,7},{6,8},{7,5},{8,6},{9,11},{10,... | collective-permute-start | bytes 786440 | tf_op jit(solution)/shard_map/ppermute | solution.py:203
  33.8 8.8 %collective-permute-start.6 = (bf16[1024,128]{1,0:T(8,128)(2,1)S(1)}, bf16[1024,128]{1,0:T(8,128)(2,1)S(1)}, u32[]{:S(2)}, u32[]{:S(2)}) collective-permute-start(bf16[1024,128]{1,0:T(8,128)(2,1)S(1)} %collective-permute-done.4.kv_ref.refs_2_), channel_id=1, source_target_pairs={{0,14},{1,3},{2,4},{3,1},{4,2},{5,7},{6,8},{7,5},{8,6},{9,11},{10,... | collective-permute-start | bytes 786440 | tf_op jit(solution)/shard_map/ppermute | solution.py:203
  38.1 8.5 %collective-permute-start.5 = (bf16[1024,128]{1,0:T(8,128)(2,1)S(1)}, bf16[1024,128]{1,0:T(8,128)(2,1)S(1)}, u32[]{:S(2)}, u32[]{:S(2)}) collective-permute-start(bf16[1024,128]{1,0:T(8,128)(2,1)S(1)} %collective-permute-done.2.kv_ref.refs_3_), channel_id=1, source_target_pairs={{0,2},{1,15},{2,0},{3,5},{4,6},{5,3},{6,4},{7,9},{8,10},{9,7},{10,... | collective-permute-start | bytes 786440 | tf_op jit(solution)/shard_map/ppermute | solution.py:203
  42.7 6.8 %collective-permute-start.8 = (bf16[1024,128]{1,0:T(8,128)(2,1)S(1)}, bf16[1024,128]{1,0:T(8,128)(2,1)S(1)}, u32[]{:S(2)}, u32[]{:S(2)}) collective-permute-start(bf16[1024,128]{1,0:T(8,128)(2,1)S(1)} %collective-permute-done.6.kv_ref.refs_4_), channel_id=1, source_target_pairs={{0,2},{1,15},{2,0},{3,5},{4,6},{5,3},{6,4},{7,9},{8,10},{9,7},{10,... | collective-permute-start | bytes 786440 | tf_op jit(solution)/shard_map/ppermute | solution.py:203
  46.7 6.9 %collective-permute-start.7 = (bf16[1024,128]{1,0:T(8,128)(2,1)S(1)}, bf16[1024,128]{1,0:T(8,128)(2,1)S(1)}, u32[]{:S(2)}, u32[]{:S(2)}) collective-permute-start(bf16[1024,128]{1,0:T(8,128)(2,1)S(1)} %collective-permute-done.5.kv_ref.refs_5_), channel_id=1, source_target_pairs={{0,14},{1,3},{2,4},{3,1},{4,2},{5,7},{6,8},{7,5},{8,6},{9,11},{10,... | collective-permute-start | bytes 786440 | tf_op jit(solution)/shard_map/ppermute | solution.py:203
  108.2 14.2 %copy-start = (bf16[1024,1024]{1,0:T(8,128)(2,1)S(1)}, bf16[1024,1024]{1,0:T(8,128)(2,1)}, u32[]{:S(2)}) copy-start(bf16[1024,1024]{1,0:T(8,128)(2,1)} %w_ref.1) | copy-start | bytes 6291460
  108.3 3.7 %collective-permute-start.9 = (f32[1024,128]{1,0:T(8,128)S(1)}, f32[1024,128]{1,0:T(8,128)S(1)}, u32[]{:S(2)}, u32[]{:S(2)}) collective-permute-start(f32[1024,128]{1,0:T(8,128)S(1)} %get-tuple-element.33), channel_id=1, source_target_pairs={{0,1},{1,0},{2,3},{3,2},{4,5},{5,4},{6,7},{7,6},{8,9},{9,8},{10,11... | collective-permute-start | bytes 1572872 | tf_op jit(solution)/shard_map/ppermute | solution.py:240
